TPU v7x, 32 devices: a whole 2x2x4 slice. The times are simulated.
32 devices in a mesh: dp: 4 (over z), blk: 8 (over y, x, core).
Axes of the slice: x: 2, y: 2, z: 4, core: 2. Of those that a mesh axis runs over, the one named last changes fastest.
Arguments:
- inputs: bfloat16 [16, 1024, 1024], P('dp', 'blk'), may hold values from -6 to 6
- mask_pos: int32 [16, 307], P('dp'), may hold values from 0 to 1023, as said below
- mask_count: int32 [16], P('dp'), may hold values from 51 to 307, as said below
- replace: bfloat16 [16, 307, 1024], P('dp'), may hold values from -6 to 6
- cotangent: bfloat16 [16, 307, 1024], P('dp'), may hold values from -6 to 6
- query_weight: bfloat16 [1024, 1024], replicated, may hold values from -0.1875 to 0.1875
- query_bias: bfloat16 [1024], replicated, may hold values from -3 to 3
- key_weight: bfloat16 [1024, 1024], replicated, may hold values from -0.1875 to 0.1875
- value_weight: bfloat16 [1024, 1024], replicated, may hold values from -0.1875 to 0.1875
- value_bias: bfloat16 [1024], replicated, may hold values from -3 to 3
- out_weight: bfloat16 [1024, 1024], replicated, may hold values from -0.375 to 0.375
- out_bias: bfloat16 [1024], replicated, may hold values from -3 to 3
- first_gain: bfloat16 [1024], replicated, may hold values from 0.099609375 to 1.8984375
- first_shift: bfloat16 [1024], replicated, may hold values from -3 to 3
- inner_weight: bfloat16 [1024, 4096], replicated, may hold values from -0.1875 to 0.1875
- inner_bias: bfloat16 [4096], replicated, may hold values from -3 to 3
- outer_weight: bfloat16 [4096, 1024], replicated, may hold values from -0.09375 to 0.09375
- outer_bias: bfloat16 [1024], replicated, may hold values from -3 to 3
- second_gain: bfloat16 [1024], replicated, may hold values from 0.099609375 to 1.8984375
- second_shift: bfloat16 [1024], replicated, may hold values from -3 to 3
Outputs:
- layer_out: float32 [16, 1024, 1024], P('dp', 'blk')
- input_grad: float32 [16, 1024, 1024], P('dp', 'blk')
- query_weight_grad: float32 [1024, 1024], P(('dp', 'blk'))
- query_bias_grad: float32 [1024], P(('dp', 'blk'))
- key_weight_grad: float32 [1024, 1024], P(('dp', 'blk'))
- value_weight_grad: float32 [1024, 1024], P(('dp', 'blk'))
- value_bias_grad: float32 [1024], P(('dp', 'blk'))
- out_weight_grad: float32 [1024, 1024], P(('dp', 'blk'))
- out_bias_grad: float32 [1024], P(('dp', 'blk'))
- first_gain_grad: float32 [1024], P(('dp', 'blk'))
- first_shift_grad: float32 [1024], P(('dp', 'blk'))
- inner_weight_grad: float32 [1024, 4096], P(('dp', 'blk'))
- inner_bias_grad: float32 [4096], P(('dp', 'blk'))
- outer_weight_grad: float32 [4096, 1024], P(('dp', 'blk'))
- outer_bias_grad: float32 [1024], P(('dp', 'blk'))
- second_gain_grad: float32 [1024], P(('dp', 'blk'))
- second_shift_grad: float32 [1024], P(('dp', 'blk'))
Inputs may be any that keep to these rules, and one draw needn't show every extreme that they name: `mask_pos`: row s lists distinct positions of sequence s; only its first mask_count[s] slots are in use. `mask_count`: slots in use of each sequence's list; some sequence uses all 307.
All inputs are finite; a program needn't handle non-finite values.
Results may differ from a plain program's by a relative error of at most 0.018.
Values may be sent and summed in bfloat16 or wider, within the bound.
No kernel may reach another device: no remote copies, remote signals or barrier semaphores. Data moves between devices by JAX's collectives and lax.ppermute only.
A program may use at most 320 MiB of HBM per device.

v0:
```python
import functools
import math

import jax
import jax.numpy as jnp
from jax import lax
from jax.experimental import pallas as pl
from jax.experimental.pallas import tpu as pltpu
from jax.sharding import PartitionSpec as P

HEAD = 64
EPSILON = 1e-05
BOTH = ("dp", "blk")
LOW = jnp.bfloat16
FULL = jnp.float32
CHUNK = 256
BACK = 512
LINES = 128
CHEAP = pl.CostEstimate(flops=1, bytes_accessed=1, transcendentals=0)


def product(left, right):
    return jnp.dot(left, right, preferred_element_type=FULL)


def right_product(left, right):
    return lax.dot_general(left, right, (((1,), (1,)), ((), ())), preferred_element_type=FULL)


def norm_stats(hidden):
    center = hidden - jnp.mean(hidden, axis=-1, keepdims=True)
    spread = jnp.mean(center * center, axis=-1, keepdims=True)
    factor = lax.rsqrt(spread + EPSILON)
    return center * factor, factor


def norm_pull(unit, factor, gain, grad):
    scaled = grad * gain
    inner = jnp.mean(scaled, axis=-1, keepdims=True)
    along = jnp.mean(scaled * unit, axis=-1, keepdims=True)
    return factor * (scaled - inner - unit * along)


def column_sum(array):
    return jnp.sum(array, axis=0, keepdims=True)


def gelu_parts(inner):
    bell = jnp.exp(-0.5 * inner * inner)
    t = 1.0 / (1.0 + (0.3275911 * math.sqrt(0.5)) * jnp.abs(inner))
    poly = 0.5 * 1.061405429
    for c in (-1.453152027, 1.421413741, -0.284496736, 0.254829592):
        poly = poly * t + 0.5 * c
    tail = poly * t * bell
    below = jnp.where(inner >= 0.0, 1.0 - tail, tail)
    return inner * below, below + inner * bell * (1.0 / math.sqrt(2.0 * math.pi))


def params(mib=40):
    return pltpu.CompilerParams(vmem_limit_bytes=mib << 20)


def forward_kernel(query_ref, key_ref, value_ref, mixed_ref, log_ref):
    lane = lax.broadcasted_iota(jnp.int32, (1, 2 * HEAD), 1)
    query = query_ref[...] * LOW(1.0 / math.sqrt(HEAD))
    key = key_ref[...]
    value_t = value_ref[...].T
    outs = []
    for head in range(2):
        mine = (lane < HEAD) if head == 0 else (lane >= HEAD)
        scores = right_product(key, jnp.where(mine, query, LOW(0)))
        highest = jnp.max(scores, axis=0, keepdims=True)
        expon = jnp.exp(scores - highest)
        total = jnp.sum(expon, axis=0, keepdims=True)
        out = product(value_t[head * HEAD : (head + 1) * HEAD], expon.astype(LOW))
        outs.append(out * (1.0 / total))
        log_ref[0, head : head + 1, :] = highest + jnp.log(total)
    mixed_ref[...] = jnp.concatenate(outs, axis=0).T.astype(LOW)


def backward_kernel(
    members, query_ref, key_ref, value_ref, mixed_ref, log_ref, *refs
):
    grads = refs[:members]
    out_ref, key_sum, value_sum = refs[-3:]
    step = pl.program_id(1)

    @pl.when(step == 0)
    def _():
        key_sum[...] = jnp.zeros_like(key_sum)
        value_sum[...] = jnp.zeros_like(value_sum)

    scale = 1.0 / math.sqrt(HEAD)
    lane = lax.broadcasted_iota(jnp.int32, (1, 2 * HEAD), 1)
    query = query_ref[...] * LOW(scale)
    key = key_ref[...]
    value = value_ref[...]
    tile = query.shape[0]
    together = tile // grads[0].shape[0]
    pieces = []
    for k in range(together):
        piece = grads[k][...]
        for other in range(k + together, members, together):
            piece = jnp.where(step == other // together, grads[other][...], piece)
        pieces.append(piece)
    grad = jnp.concatenate(pieces, axis=0)
    both = (grad.astype(FULL) * mixed_ref[...].astype(FULL)).T
    key_t = key.T
    outs = []
    for head in range(2):
        mine = (lane < HEAD) if head == 0 else (lane >= HEAD)
        own = slice(head * HEAD, (head + 1) * HEAD)
        delta = jnp.sum(both[own], axis=0, keepdims=True)
        query_one = jnp.where(mine, query, LOW(0))
        grad_one = jnp.where(mine, grad, LOW(0))
        shares = jnp.exp(right_product(key, query_one) - log_ref[0, head : head + 1, :])
        grad_shares = right_product(value, grad_one)
        grad_scores = (shares * (grad_shares - delta)).astype(LOW)
        value_sum[...] += product(shares.astype(LOW), grad_one)
        key_sum[...] += product(grad_scores, query_one)
        outs.append(product(key_t[own], grad_scores))
    spot = pl.ds(pl.multiple_of(step * tile, tile), tile)
    out_ref[0, spot, :] = (jnp.concatenate(outs, axis=0).T * scale).astype(LOW)

    @pl.when(step == pl.num_programs(1) - 1)
    def _():
        out_ref[1] = key_sum[...].astype(LOW)
        out_ref[2] = value_sum[...].astype(LOW)


def attention_forward(joined):
    rows, wide = joined.shape
    share = wide // 3
    pairs = share // (2 * HEAD)
    tile = min(1024, rows)

    def whole(offset):
        return pl.BlockSpec((rows, 2 * HEAD), lambda p, i: (0, offset + p))

    line = pl.BlockSpec((tile, 2 * HEAD), lambda p, i: (i, p))
    return pl.pallas_call(
        forward_kernel,
        grid=(pairs, rows // tile),
        in_specs=[line, whole(pairs), whole(2 * pairs)],
        out_specs=[line, pl.BlockSpec((1, 2, tile), lambda p, i: (p, 0, i))],
        out_shape=[
            jax.ShapeDtypeStruct((rows, share), LOW),
            jax.ShapeDtypeStruct((pairs, 2, rows), FULL),
        ],
        compiler_params=params(48),
        cost_estimate=CHEAP,
        name="attention_forward",
    )(joined, joined, joined)


def attention_backward(joined, grad_mixed, mixed, log_total, first, count, previous=None):
    rows, wide = joined.shape
    share = wide // 3
    pairs = share // (2 * HEAD)
    members = len(grad_mixed)
    own_rows = rows // members
    tile = own_rows * max(1, BACK // own_rows)

    def whole(offset):
        return pl.BlockSpec((rows, 2 * HEAD), lambda p, i: (0, offset + p))

    line = pl.BlockSpec((tile, 2 * HEAD), lambda p, i: (i, first + p))
    grad_line = pl.BlockSpec((own_rows, 2 * HEAD), lambda p, i: (0, first + p))
    more = [] if previous is None else [previous]
    return pl.pallas_call(
        functools.partial(backward_kernel, members),
        grid=(count, rows // tile),
        in_specs=[
            line,
            whole(pairs + first),
            whole(2 * pairs + first),
            line,
            pl.BlockSpec((1, 2, tile), lambda p, i: (first + p, 0, i)),
        ]
        + [grad_line] * members
        + [pl.BlockSpec(memory_space=pl.ANY)] * len(more),
        out_specs=pl.BlockSpec((3, rows, 2 * HEAD), lambda p, i: (0, 0, first + p)),
        out_shape=jax.ShapeDtypeStruct((3, rows, share), LOW),
        input_output_aliases={5 + members: 0} if more else {},
        scratch_shapes=[pltpu.VMEM((rows, 2 * HEAD), FULL)] * 2,
        compiler_params=params(48),
        cost_estimate=CHEAP,
        name="attention_backward",
    )(joined, joined, joined, mixed, log_total, *grad_mixed, *more)


def rows_kernel(sequence_ref, count_ref, position_ref, listed_ref, replace_ref, cotangent_ref, *refs):
    swapped_ref, seeded_ref, masked_ref = refs
    count = count_ref[sequence_ref[0]]
    listed = listed_ref[0]
    live = lax.broadcasted_iota(jnp.int32, listed.shape, 1) < count
    matches = jnp.where(live, listed, -1) == position_ref[...]
    select = matches.astype(FULL)
    masked_ref[...] = jnp.max(select, axis=1, keepdims=True)
    select = select.astype(LOW)
    swapped_ref[...] = product(select, replace_ref[0]).astype(LOW)
    seeded_ref[...] = product(select, cotangent_ref[0]).astype(LOW)


def masked_rows(sequence, mask_count, positions, mask_pos, replace, cotangent):
    rows = positions.shape[0]
    _, slots, width = replace.shape
    line = pl.BlockSpec((1, slots, width), lambda i, s, c: (s[0], 0, 0))
    return pl.pallas_call(
        rows_kernel,
        grid_spec=pltpu.PrefetchScalarGridSpec(
            num_scalar_prefetch=2,
            grid=(1,),
            in_specs=[
                pl.BlockSpec((rows, 1), lambda i, s, c: (0, 0)),
                pl.BlockSpec((1, 1, slots), lambda i, s, c: (s[0], 0, 0)),
                line,
                line,
            ],
            out_specs=[
                pl.BlockSpec((rows, width), lambda i, s, c: (0, 0)),
                pl.BlockSpec((rows, width), lambda i, s, c: (0, 0)),
                pl.BlockSpec((rows, 1), lambda i, s, c: (0, 0)),
            ],
        ),
        out_shape=[
            jax.ShapeDtypeStruct((rows, width), LOW),
            jax.ShapeDtypeStruct((rows, width), LOW),
            jax.ShapeDtypeStruct((rows, 1), FULL),
        ],
        compiler_params=params(),
        cost_estimate=CHEAP,
        name="masked_rows",
    )(sequence, mask_count, positions, mask_pos.reshape(-1, 1, slots), replace, cotangent)


def first_kernel(pieces, current_ref, bias_ref, gain_ref, shift_ref, *refs):
    mixed, weights = refs[:pieces], refs[pieces : 2 * pieces]
    first_ref, flip_ref, low_ref, unit_ref, factor_ref = refs[2 * pieces :]
    total = current_ref[...].astype(FULL) + bias_ref[...].astype(FULL)
    for part, weight in zip(mixed, weights):
        total = total + product(part[...], weight[...])
    unit, factor = norm_stats(total)
    first = unit * gain_ref[...].astype(FULL) + shift_ref[...].astype(FULL)
    first_ref[...] = first
    low = first.astype(LOW)
    low_ref[...] = low
    flip_ref[...] = low.T
    unit_ref[...] = unit
    factor_ref[...] = factor


def row_of(k, width):
    return pl.BlockSpec((None, 1, width), lambda *_: (k, 0, 0))


def first_half(current, mixed, weights, small):
    rows, width = current.shape
    tile = 128
    pieces = len(mixed)
    line = pl.BlockSpec((tile, width), lambda i: (i, 0))
    return pl.pallas_call(
        functools.partial(first_kernel, pieces),
        grid=(rows // tile,),
        in_specs=[line] + [row_of(k, width) for k in (0, 1, 2)]
        + [pl.BlockSpec((tile, block_width), lambda i: (i, 0)) for _, block_width in mixed]
        + [pl.BlockSpec(w.shape, lambda i: (0, 0)) for w in weights],
        out_specs=[
            line,
            pl.BlockSpec((width, tile), lambda i: (0, i)),
            line,
            line,
            pl.BlockSpec((tile, 1), lambda i: (i, 0)),
        ],
        out_shape=[
            jax.ShapeDtypeStruct((rows, width), FULL),
            jax.ShapeDtypeStruct((width, rows), LOW),
            jax.ShapeDtypeStruct((rows, width), LOW),
            jax.ShapeDtypeStruct((rows, width), FULL),
            jax.ShapeDtypeStruct((rows, 1), FULL),
        ],
        compiler_params=params(60),
        cost_estimate=CHEAP,
        name="first_half",
    )(current, small, small, small, *[m for m, _ in mixed], *weights)


def feed_kernel(
    size, unit_rows, place_ref, low_ref, first_ref, seed_ref, inner_ref, inner_bias_ref, outer_ref,
    outer_bias_ref, gain_ref, shift_ref, *refs,
):
    actives = refs[:size]
    slope_ref, result_ref, grad_ref, grad_low_ref, sums_ref, acc, flip = refs[size:]
    step = pl.program_id(0)
    inner = product(low_ref[...], inner_ref[...]) + inner_bias_ref[...].astype(FULL)
    active, slope = gelu_parts(inner)
    active = active.astype(LOW)
    slope_ref[...] = slope.astype(LOW)
    flip[...] = active.T
    rank = place_ref[1]
    tile = flip.shape[0]
    for k in range(size):
        for q in range(tile // (unit_rows * size)):
            line = pl.multiple_of((q * size + (rank ^ k)) * unit_rows, 16)
            actives[k][q * unit_rows : (q + 1) * unit_rows, :] = flip[pl.ds(line, unit_rows), :]
    part = product(active, outer_ref[...])

    @pl.when(step == 0)
    def _():
        acc[...] = part

    @pl.when(step > 0)
    def _():
        acc[...] += part

    @pl.when(step == pl.num_programs(0) - 1)
    def _():
        gain = gain_ref[...].astype(FULL)
        shift = shift_ref[...].astype(FULL)
        bias = outer_bias_ref[...].astype(FULL)

        def some(block, sums):
            lines = pl.ds(pl.multiple_of(block * LINES, LINES), LINES)
            unit, factor = norm_stats(first_ref[lines, :] + acc[lines, :] + bias)
            result_ref[lines, :] = (unit * gain + shift).astype(LOW)
            seed = seed_ref[lines, :].astype(FULL)
            grad = norm_pull(unit, factor, gain, seed)
            grad_ref[lines, :] = grad
            grad_low_ref[lines, :] = grad.astype(LOW)
            more = (column_sum(seed * unit), column_sum(seed), column_sum(grad))
            return tuple(x + y for x, y in zip(sums, more))

        sums = lax.fori_loop(0, acc.shape[0] // LINES, some, (jnp.zeros_like(gain),) * 3)
        for k in range(3):
            sums_ref[k : k + 1, :] = sums[k]


def feed_forward(
    places, size, number, low, first, seeded, inner_weight, inner_bias, outer_weight, small
):
    rows, width = low.shape
    hidden = inner_weight.shape[1]
    tile = 512
    whole = pl.BlockSpec((rows, width), lambda i, s: (0, 0))
    across = pl.BlockSpec((rows, tile), lambda i, s: (0, i))
    return pl.pallas_call(
        functools.partial(feed_kernel, size, hidden // number),
        grid_spec=pltpu.PrefetchScalarGridSpec(
            num_scalar_prefetch=1,
            grid=(hidden // tile,),
            in_specs=[
                whole,
                whole,
                whole,
                pl.BlockSpec((width, tile), lambda i, s: (0, i)),
                pl.BlockSpec((1, tile), lambda i, s: (0, i)),
                pl.BlockSpec((tile, width), lambda i, s: (i, 0)),
            ]
            + [row_of(k, width) for k in (3, 4, 5)],
            out_specs=[pl.BlockSpec((tile // size, rows), lambda i, s: (i, 0))] * size
            + [across, whole, whole, whole, pl.BlockSpec((8, width), lambda i, s: (0, 0))],
            scratch_shapes=[pltpu.VMEM((rows, width), FULL), pltpu.VMEM((tile, rows), LOW)],
        ),
        out_shape=[jax.ShapeDtypeStruct((hidden // size, rows), LOW)] * size
        + [
            jax.ShapeDtypeStruct((rows, hidden), LOW),
            jax.ShapeDtypeStruct((rows, width), LOW),
            jax.ShapeDtypeStruct((rows, width), FULL),
            jax.ShapeDtypeStruct((rows, width), LOW),
            jax.ShapeDtypeStruct((8, width), FULL),
        ],
        compiler_params=params(60),
        cost_estimate=CHEAP,
        name="feed_forward",
    )(places, low, first, seeded, inner_weight, inner_bias, outer_weight, small, small, small)


def feed_back_kernel(
    size, steps, share, place_ref, grad_low_ref, grad_ref, slope_ref, inner_ref, outer_ref, unit_ref,
    factor_ref, gain_ref, *refs,
):
    out_weights, refs = refs[:size], refs[size:]
    inners = refs[:size]
    bias_ref, one_ref, low_ref, sums_ref = refs[size : size + 4]
    cuts = refs[size + 4 : 2 * size + 4]
    mixes = refs[2 * size + 4 : 3 * size + 4]
    acc, keep = refs[3 * size + 4 :]
    step = pl.program_id(0)
    grad_inner = slope_ref[...].astype(FULL) * right_product(grad_low_ref[...], outer_ref[...])
    bias_ref[...] = column_sum(grad_inner)
    grad_inner = grad_inner.astype(LOW)
    for k in range(size):

        @pl.when(step // steps == (k + size - 1) % size)
        def _():
            inners[k][...] = grad_inner

    part = right_product(grad_inner, inner_ref[...])

    @pl.when(step == 0)
    def _():
        acc[...] = part

    @pl.when(step > 0)
    def _():
        acc[...] += part

    @pl.when(step == pl.num_programs(0) - 1)
    def _():
        gain = gain_ref[...].astype(FULL)

        def some(block, sums):
            lines = pl.ds(pl.multiple_of(block * LINES, LINES), LINES)
            grad = grad_ref[lines, :] + acc[lines, :]
            unit = unit_ref[lines, :]
            one = norm_pull(unit, factor_ref[lines, :], gain, grad)
            one_ref[lines, :] = one
            low = one.astype(LOW)
            low_ref[lines, :] = low
            keep[lines, :] = low
            more = (column_sum(grad * unit), column_sum(grad), column_sum(one))
            return tuple(x + y for x, y in zip(sums, more))

        sums = lax.fori_loop(0, acc.shape[0] // LINES, some, (jnp.zeros_like(gain),) * 3)
        for k in range(3):
            sums_ref[k : k + 1, :] = sums[k]
        low = keep[...]
        for k in range(size):
            spot = pl.multiple_of((place_ref[1] ^ k) * share, 128)
            cuts[k][...] = keep[:, pl.ds(spot, share)]
            mixes[k][...] = right_product(low, out_weights[k][...]).astype(LOW)


def feed_back(
    places, size, grad_low, grad, slope, inner_weight, outer_weight, unit, factor, small, out_weights
):
    rows, width = grad_low.shape
    hidden = inner_weight.shape[1]
    part = hidden // size
    tile = min(512, part)
    steps = part // tile
    share = width // size

    def spot(i, s):
        return (s[1] ^ ((i // steps + 1) % size)) * steps + i % steps

    def own(k):
        start = ((k + size - 1) % size) * steps
        return pl.BlockSpec((rows, tile), lambda i, s: (0, jnp.clip(i - start, 0, steps - 1)))

    whole = pl.BlockSpec((rows, width), lambda i, s: (0, 0))
    return pl.pallas_call(
        functools.partial(feed_back_kernel, size, steps, share),
        grid_spec=pltpu.PrefetchScalarGridSpec(
            num_scalar_prefetch=1,
            grid=(hidden // tile,),
            in_specs=[
                whole,
                whole,
                pl.BlockSpec((rows, tile), lambda i, s: (0, spot(i, s))),
                pl.BlockSpec((width, tile), lambda i, s: (0, spot(i, s))),
                pl.BlockSpec((tile, width), lambda i, s: (spot(i, s), 0)),
                whole,
                pl.BlockSpec((rows, 1), lambda i, s: (0, 0)),
                row_of(1, width),
            ]
            + [pl.BlockSpec((share, width), lambda i, s: (0, 0))] * size,
            out_specs=[own(k) for k in range(size)]
            + [
                pl.BlockSpec((1, tile), lambda i, s: (0, spot(i, s))),
                whole,
                whole,
                pl.BlockSpec((8, width), lambda i, s: (0, 0)),
            ]
            + [pl.BlockSpec((rows, share), lambda i, s: (0, 0))] * (2 * size),
            scratch_shapes=[pltpu.VMEM((rows, width), FULL), pltpu.VMEM((rows, width), LOW)],
        ),
        out_shape=[jax.ShapeDtypeStruct((rows, part), LOW)] * size
        + [
            jax.ShapeDtypeStruct((1, hidden), FULL),
            jax.ShapeDtypeStruct((rows, width), FULL),
            jax.ShapeDtypeStruct((rows, width), LOW),
            jax.ShapeDtypeStruct((8, width), FULL),
        ]
        + [jax.ShapeDtypeStruct((rows, share), LOW)] * (2 * size),
        compiler_params=params(60),
        cost_estimate=CHEAP,
        name="feed_back",
    )(places, grad_low, grad, slope, inner_weight, outer_weight, unit, factor, small, *out_weights)


def back_kernel(size, place_ref, grad_ref, masked_ref, *refs):
    threes, weights, out_ref = refs[:size], refs[size:-1], refs[-1]
    total = grad_ref[...]
    for k in range(size):
        for n in range(3):
            total = total + right_product(threes[k][n], weights[3 * k + n][...])
    out_ref[...] = jnp.where(masked_ref[...] > 0.0, 0.0, total).astype(LOW)


def input_back(places, threes, weights, grad, masked):
    size = len(threes)
    rows, width = grad.shape
    share = threes[0].shape[2]
    tile = min(256, rows)
    line = pl.BlockSpec((tile, width), lambda i, s: (i, 0))
    return pl.pallas_call(
        functools.partial(back_kernel, size),
        grid_spec=pltpu.PrefetchScalarGridSpec(
            num_scalar_prefetch=1,
            grid=(rows // tile,),
            in_specs=[line, pl.BlockSpec((tile, 1), lambda i, s: (i, 0))]
            + [pl.BlockSpec((3, tile, share), lambda i, s: (0, i, 0))] * size
            + [
                pl.BlockSpec((width, share), lambda i, s, k=k: (0, s[1] ^ k))
                for k in range(size)
                for _ in range(3)
            ],
            out_specs=line,
        ),
        out_shape=jax.ShapeDtypeStruct((rows, width), LOW),
        compiler_params=params(),
        cost_estimate=CHEAP,
        name="input_back",
    )(places, grad, masked, *threes, *(list(weights) * size))


def part_orders(bits):
    if bits < 3:
        return [(list(range(bits)),) * 2] * 2
    rest = list(range(3, bits))
    return [([0, 2, 1] + rest, [1, 0, 2] + rest), ([2, 1, 0] + rest,) * 2]


def part_depths(lines, weights):
    tiles = lines // 16
    first = round(tiles * weights[0] / sum(weights))
    return [16 * first, 16 * (tiles - first)]


def offset_at(position, order):
    return sum(((position >> (len(order) - 1 - n)) & 1) << order[n] for n in range(len(order)))


def weight_kernel(layout, flips, teams, lines, parts, members, bias, extra, place_ref, *refs):
    number = sum(layout)
    lefts, rights = refs[:number], refs[number : number + members]
    count = 2 * len(parts)
    singles, refs = refs[number + members : number + members + extra], refs[number + members + extra :]
    outs, scratch = refs[:count], refs[count:]
    flipped = scratch[:members] if flips else lefts
    total = scratch[members if flips else 0]
    step = pl.program_id(0)
    team = place_ref[0]
    half = teams // 2

    def block_at(position, order):
        even, odd = (offset_at(position, o) for o in order)
        return team ^ (even if even == odd else jnp.where(place_ref[1] % 2 == 0, even, odd))

    if flips:

        @pl.when(step == 0)
        def _():
            spot = 0
            for member in range(members):
                start = 0
                for _ in range(layout[member]):
                    wide = lefts[spot].shape[1]
                    flipped[member][start : start + wide, :] = lefts[spot][...].T
                    start, spot = start + wide, spot + 1

    def right(member):
        ref = rights[member]
        return ref[0] if len(ref.shape) == 3 else ref[...]

    def multiply():
        acc = product(flipped[0][...], right(0))
        for member in range(1, members):
            acc = acc + product(flipped[member][...], right(member))
        total[...] = acc.astype(LOW)
        for k, (order, start, deep) in enumerate(parts):
            for position in range(teams):
                line = pl.multiple_of(block_at(position, order) * lines + start, 16)
                outs[2 * k + position // half][position % half, 0] = total[pl.ds(line, deep), :]

    if not bias and not extra:
        multiply()
        return

    chunks = pl.num_programs(0) - 1
    last = outs[count - 2 : count]
    order = parts[-1][0]
    if extra:
        vectors = scratch[-1]

        @pl.when(step < chunks)
        def _():
            multiply()

        @pl.when(step == chunks)
        def _():
            inner = singles[-1].shape[1] // teams
            for row in range(teams):
                for k in range(6):
                    vectors[row : row + 1, k * lines : (k + 1) * lines] = singles[k // 3][
                        k % 3 : k % 3 + 1, row * lines : (row + 1) * lines
                    ]
                vectors[row : row + 1, 6 * lines : 6 * lines + inner] = singles[2][
                    :, row * inner : (row + 1) * inner
                ]
            deep = lax.broadcasted_iota(jnp.int32, (16, CHUNK), 0)
            for position in range(teams):
                row = vectors[pl.ds(block_at(position, order), 1), :]
                value = jnp.zeros((16, CHUNK), FULL)
                for k in range(vectors.shape[1] // CHUNK):
                    piece = jnp.broadcast_to(row[:, k * CHUNK : (k + 1) * CHUNK], (16, CHUNK))
                    value = jnp.where(deep == k, piece, value)
                last[position // half][position % half, 0, 0:16, :] = value.astype(LOW)

        return

    sums, vectors = scratch[-2:]

    @pl.when(step < chunks)
    def _():
        multiply()
        sums[pl.ds(step, 1), :] = sum(column_sum(right(m).astype(FULL)) for m in range(members))

    @pl.when(step == chunks)
    def _():
        own = vectors.shape[0]
        for k, first in enumerate(bias[0]):
            for team_row in range(own):
                chunk, lane = divmod(first + team_row * lines, CHUNK)
                vectors[team_row : team_row + 1, k * lines : (k + 1) * lines] = sums[
                    chunk : chunk + 1, lane : lane + lines
                ]
        wide = vectors.shape[1]
        for position in range(teams):
            local = block_at(position, order) - place_ref[1] * (teams // members) - bias[1]
            inside = jnp.logical_and(local >= 0, local < own)
            row = vectors[pl.ds(jnp.clip(local, 0, own - 1), 1), :]
            row = jnp.where(inside, row, 0.0)
            last[position // half][position % half, 0, 0:16, 0:wide] = jnp.broadcast_to(
                row, (16, wide)
            ).astype(LOW)


def weight_grad(name, lefts, flips, rights, places, teams, width, weights, bias=(), sums=(), mib=60):
    members = len(lefts)
    rows = rights[0][1][-2]
    flat = [item for member in lefts for item in member]
    high = sum(a.shape[1] for a, _ in lefts[0]) if flips else lefts[0][0][0].shape[0]
    lines = high // teams
    orders = part_orders(teams.bit_length() - 1)
    parts, start = [], 0
    for order, deep in zip(orders, part_depths(lines, weights)):
        if deep:
            parts.append((order, start, deep))
        start += deep
    half = teams // 2
    chunks = width // CHUNK
    own = bias[2] if bias else 0
    if sums:
        sums_wide = 6 * lines + sums[-1].shape[1] // teams
        sums_wide = -(-sums_wide // CHUNK) * CHUNK
    counts = [chunks] * len(parts)
    if bias or sums:
        counts[-1] += 1
    outs = pl.pallas_call(
        functools.partial(
            weight_kernel, [len(m) for m in lefts], flips, teams, lines, parts, members, bias, len(sums)
        ),
        grid_spec=pltpu.PrefetchScalarGridSpec(
            num_scalar_prefetch=1,
            grid=(counts[-1],),
            in_specs=[
                pl.BlockSpec(
                    (rows, array.shape[1]) if flips else array.shape, lambda i, s, b=block: (b, 0)
                )
                for array, block in flat
            ]
            + [
                pl.BlockSpec(shape, lambda i, s, f=index: f(jnp.minimum(i, chunks - 1), s))
                for _, shape, index in rights
            ]
            + [pl.BlockSpec(a.shape, lambda i, s: (0, 0)) for a in sums],
            out_specs=[
                pl.BlockSpec(
                    (half, 1, p[2], CHUNK), lambda i, s, c=c: (0, jnp.minimum(i, c - 1), 0, 0)
                )
                for p, c in zip(parts, counts)
                for _ in range(2)
            ],
            scratch_shapes=[pltpu.VMEM((high, rows), LOW)] * (members if flips else 0)
            + [pltpu.VMEM((high, CHUNK), LOW)]
            + (
                [pltpu.VMEM((chunks, CHUNK), FULL), pltpu.VMEM((own, len(bias[0]) * lines), FULL)]
                if bias
                else [pltpu.VMEM((teams, sums_wide), FULL)] if sums else []
            ),
        ),
        out_shape=[
            jax.ShapeDtypeStruct((half, c, p[2], CHUNK), LOW)
            for p, c in zip(parts, counts)
            for _ in range(2)
        ],
        compiler_params=params(mib),
        cost_estimate=CHEAP,
        name="weight_grad",
    )(places, *[array for array, _ in flat], *[array for array, _, _ in rights], *sums)
    made = []
    for k, (order, start, deep) in enumerate(parts):
        near, far = (o.reshape(half, counts[k] * deep, CHUNK) for o in outs[2 * k : 2 * k + 2])
        segments = [(name, start, deep, c) for c in range(chunks)]
        if counts[k] > chunks:
            segments.append(("bias", 0, deep, 0))
        made.append(dict(order=order, near=near, far=far, segments=segments))
    return made


def fold_kernel(counts, *refs):
    total = 4 * sum(counts)
    outs = refs[total:]
    spot = 0
    for k, count in enumerate(counts):
        start = 0
        for _ in range(count):
            near_low, near_high, came_low, came_high = refs[spot : spot + 4]
            deep = near_low.shape[1]
            rows = slice(start, start + deep)
            outs[2 * k][:, rows] = (near_low[...].astype(FULL) + came_low[...].astype(FULL)).astype(LOW)
            outs[2 * k + 1][:, rows] = (
                near_high[...].astype(FULL) + came_high[...].astype(FULL)
            ).astype(LOW)
            start, spot = start + deep, spot + 4


def fold(*groups):
    orders = []
    for group in groups:
        for part in group:
            if part["order"] not in orders:
                orders.append(part["order"])
    merged = [[p for g in groups for p in g if p["order"] == order] for order in orders]
    half = merged[0][0]["near"].shape[0] // 2
    operands, in_specs, out_specs, out_shape, counts = [], [], [], [], []
    for parts in merged:
        rows = 0
        for part in parts:
            deep = part["near"].shape[1]
            rows += deep
            low = pl.BlockSpec((1, deep, CHUNK), lambda i: (i, 0, 0))
            high = pl.BlockSpec((1, deep, CHUNK), lambda i: (half + i, 0, 0))
            operands += [part["near"], part["near"], part["came"], part["came"]]
            in_specs += [low, high, low, high]
        counts.append(len(parts))
        out_specs += [pl.BlockSpec((1, rows, CHUNK), lambda i: (i, 0, 0))] * 2
        out_shape += [jax.ShapeDtypeStruct((half, rows, CHUNK), LOW)] * 2
    outs = pl.pallas_call(
        functools.partial(fold_kernel, counts),
        grid=(half,),
        in_specs=in_specs,
        out_specs=out_specs,
        out_shape=out_shape,
        compiler_params=params(60 if len(operands) > 16 else 40),
        cost_estimate=CHEAP,
        name="fold",
    )(*operands)
    return [
        dict(
            order=tuple(o[1:] for o in parts[0]["order"]),
            near=outs[2 * k],
            far=outs[2 * k + 1],
            segments=[s for p in parts for s in p["segments"]],
        )
        for k, parts in enumerate(merged)
    ]


def final_kernel(layouts, plain, settled, size, lines, place_ref, *refs):
    count = len(layouts)
    outs = refs[2 * count :]
    targets = dict(zip(plain, outs))
    pieces = outs[len(plain) : len(plain) + size]
    if settled:
        targets[None] = outs[-1]
    biases = []
    for k, layout in enumerate(layouts):
        spot = 0
        for name, start, deep, column in layout:
            rows = slice(spot, spot + (16 if name == "bias" else deep))
            value = refs[2 * k][0, rows].astype(FULL) + refs[2 * k + 1][0, rows].astype(FULL)
            spot += deep
            if name == "bias":
                biases.append(value[0:8])
                continue
            targets[name][start : start + deep, column * CHUNK : (column + 1) * CHUNK] = value
    if settled:
        for piece in pieces if biases else ():
            piece[lines : lines + 8, 0:CHUNK] = sum(biases)
        for k in range(size):
            line = pl.multiple_of((place_ref[1] ^ k) * lines, 8)
            pieces[k][0:lines, :] = targets[None][pl.ds(line, lines), :]


def final(parts, places, size, lines, plain, settled):
    layouts, wide, more = [], 0, 0
    for part in parts:
        layout = []
        for name, start, deep, column in part["segments"]:
            if name in plain or name == "bias":
                more = 8 if name == "bias" else more
                layout.append((name, start, deep, column))
            else:
                column += settled[name] // CHUNK
                wide = max(wide, (column + 1) * CHUNK)
                layout.append((None, start, deep, column))
        layouts.append(layout)
    names = list(plain)
    shapes = [jax.ShapeDtypeStruct(plain[n], FULL) for n in names]
    if settled:
        shapes += [jax.ShapeDtypeStruct((lines + more, wide), FULL)] * size
    outs = pl.pallas_call(
        functools.partial(final_kernel, layouts, names, bool(settled), size, lines),
        in_specs=[pl.BlockSpec(memory_space=pltpu.SMEM)]
        + [pl.BlockSpec(memory_space=pltpu.VMEM)] * (2 * len(parts)),
        out_specs=[pl.BlockSpec(memory_space=pltpu.VMEM)] * len(shapes),
        out_shape=shapes,
        scratch_shapes=[pltpu.VMEM((size * lines, wide), FULL)] if settled else [],
        compiler_params=params(32),
        cost_estimate=CHEAP,
        name="final",
    )(places, *[p[n] for p in parts for n in ("near", "came")])
    return dict(zip(names, outs)), outs[len(names) :]


def tie(value, *others):
    return lax.optimization_barrier((value, others))[0]


def per_device(
    inputs,
    mask_pos,
    mask_count,
    replace,
    cotangent,
    query_weight,
    query_bias,
    key_weight,
    value_weight,
    value_bias,
    out_weight,
    out_bias,
    first_gain,
    first_shift,
    inner_weight,
    inner_bias,
    outer_weight,
    outer_bias,
    second_gain,
    second_shift,
):
    groups, rows, width = inputs.shape
    hidden = inner_weight.shape[1]
    blocks = lax.axis_size("blk")
    number = lax.axis_size("dp") * blocks
    size = blocks // groups
    piece = rows // size
    own_rows = blocks * piece
    teams = number // size
    bits = teams.bit_length() - 1
    place = lax.axis_index("blk")
    flat = lax.axis_index("dp") * blocks + place
    sequence = place // size
    rank = place % size
    team = flat // size
    share = width // size
    hidden_share = hidden // size
    others = range(1, size)

    def hop(array, mask):
        return lax.ppermute(array, BOTH, [(i, i ^ mask) for i in range(number)])

    def cut(array, who, count, axis):
        return lax.dynamic_slice_in_dim(array, who * count, count, axis=axis)

    def swap(make):
        return [make(rank)] + [hop(make(rank ^ k), k) for k in others]

    def absolute(pieces, axis):
        if size == 2:
            first = rank == 0
            return jnp.concatenate(
                [jnp.where(first, pieces[0], pieces[1]), jnp.where(first, pieces[1], pieces[0])],
                axis=axis,
            )
        stacked = jnp.stack(pieces)
        return jnp.concatenate(
            [lax.dynamic_index_in_dim(stacked, q ^ rank, 0, keepdims=False) for q in range(size)],
            axis=axis,
        )

    def send(parts):
        return [
            dict(
                p,
                came=lax.ppermute(
                    p["far"],
                    BOTH,
                    [(i, i ^ (size << p["order"][i % size % 2][0])) for i in range(number)],
                ),
            )
            for p in parts
        ]

    def far(parts):
        return [p["far"] for p in parts]

    def sync(values, *groups):
        values, came = lax.optimization_barrier((values, [[p["came"] for p in g] for g in groups]))
        made = [[dict(p, came=c) for p, c in zip(g, cs)] for g, cs in zip(groups, came)]
        return (values, *made)

    def after(parts, *values):
        came = lax.optimization_barrier(([p["came"] for p in parts], values))[0]
        return [dict(p, came=c) for p, c in zip(parts, came)]

    arrived = lax.all_to_all(inputs.reshape(blocks, piece, width), "blk", 0, 0)
    lane = jnp.arange(own_rows, dtype=jnp.int32)
    positions = (lane // piece) * rows + rank * piece + lane % piece
    swapped, seeded, masked = masked_rows(
        sequence.reshape(1).astype(jnp.int32), mask_count, positions.reshape(-1, 1), mask_pos, replace, cotangent
    )
    places = jnp.stack([team, rank]).astype(jnp.int32)
    heads_weight = jnp.concatenate(
        [cut(w, rank, share, 1) for w in (query_weight, key_weight, value_weight)], axis=1
    )
    heads_bias = jnp.concatenate(
        [
            cut(query_bias, rank, share, 0),
            jnp.zeros((share,), LOW),
            cut(value_bias, rank, share, 0),
        ]
    )
    out_weights = [cut(out_weight, rank ^ k, share, 0) for k in range(size)]

    small = (out_bias, first_gain, first_shift, outer_bias, second_gain, second_shift)
    small = jnp.stack(small).astype(FULL).reshape(-1, 1, width)
    inner_line = inner_bias.reshape(1, -1)
    arrived = tie(arrived, small, inner_line, swapped, seeded, heads_weight, heads_bias, out_weights, masked)
    current = jnp.where(masked > 0.0, swapped, arrived.reshape(own_rows, width))
    currents = [current] + [hop(current, k) for k in others]
    joined = product(jnp.concatenate(currents, axis=0), heads_weight) + heads_bias.astype(FULL)
    joined = joined.astype(LOW)
    mixed_heads, log_total = attention_forward(joined)

    mixed_parts = mixed_heads.reshape(size, own_rows, share)
    mixed_here = [mixed_parts[0]] + [hop(mixed_parts[k], k) for k in others]
    mixed_away = []
    for k in others:
        row = []
        for q in range(size):
            if q == 0:
                row.append((mixed_heads, k))
            else:
                row.append((hop(mixed_parts[k ^ q], q), 0))
        mixed_away.append(row)

    first, first_flip, first_low, unit_one, factor_one = first_half(
        current,
        [(m, share) for m in [mixed_heads] + mixed_here[1:]],
        out_weights,
        small,
    )
    firsts = [first_flip] + [hop(first_flip, k) for k in others]
    fed = feed_forward(
        places, size, number, first_low, first, seeded, inner_weight, inner_line, outer_weight, small
    )
    actives = [fed[0]] + [hop(fed[k], k) for k in others]
    slope, result, grad_two, grad_two_low, second_sums = fed[size:]

    def home(array):
        return lax.all_to_all(array.reshape(blocks, piece, width), "blk", 0, 0)

    def wide(array):
        return array.reshape(groups, rows, width).astype(FULL)

    grad_twos = [grad_two_low] + [hop(grad_two_low, k) for k in others]

    def plain(array):
        return (array, (own_rows, CHUNK), lambda i, s: (0, i))

    layer_out = home(result)
    back = feed_back(
        places, size, grad_two_low, grad_two, slope, inner_weight, outer_weight, unit_one, factor_one,
        small, out_weights,
    )
    back, layer_out, grad_twos, actives = lax.optimization_barrier((back, layer_out, grad_twos, actives))
    layer_out = wide(layer_out)
    grad_inners = [back[0]] + [hop(back[k], k) for k in others]
    inner_bias_grad, grad_one, grad_one_low, first_sums = back[size : size + 4]
    grad_ones = [back[size + 4]] + [hop(back[size + 4 + k], k) for k in others]
    grad_mixed = back[2 * size + 4 : 3 * size + 4]
    grad_mixed = [grad_mixed[0]] + [hop(grad_mixed[k], k) for k in others]
    outer_parts = weight_grad(
        "outer", [[(a, 0)] for a in actives], False, [plain(g) for g in grad_twos], places, teams, width,
        (2, 1),
    )
    grad_ones[0] = tie(grad_ones[0], far(outer_parts))
    outer_parts = send(outer_parts)
    out_parts = weight_grad(
        "out", [[(m, 0) for m in [mixed_heads] + mixed_here[1:]]] + mixed_away, True,
        [plain(g) for g in grad_ones],
        jnp.stack([team ^ (rank * (teams // size)), rank]).astype(jnp.int32), teams, share, (1, 0),
    )
    grad_inners[0] = tie(grad_inners[0], far(out_parts))
    out_parts = send(out_parts)
    inner_parts = weight_grad(
        "inner", [[(f, 0)] for f in firsts], False, [plain(g) for g in grad_inners], places, teams,
        hidden_share, (3, 1), sums=(first_sums, second_sums, inner_bias_grad),
    )
    fars, outer_parts = sync(far(inner_parts), outer_parts)
    inner_parts = send([dict(p, far=f) for p, f in zip(inner_parts, fars)])
    grad_mixed[0] = tie(grad_mixed[0], fars)

    pairs = share // (2 * HEAD)
    number_of = 2 if share // 2 % CHUNK == 0 else 1
    count = pairs // number_of
    part = share // number_of
    chunks = part // CHUNK
    team_rows = teams // size // number_of

    def three_grad(three, group):
        return weight_grad(
            f"three{group}", [[(c, 0)] for c in currents], True,
            [
                (
                    three,
                    (1, own_rows, CHUNK),
                    lambda i, s, k=k: (i // chunks, k, group * chunks + i % chunks),
                )
                for k in range(size)
            ],
            places, teams, 3 * part, (3, 1), ((0, 2 * part), group * team_rows, team_rows), mib=40,
        )

    three = attention_backward(joined, grad_mixed, mixed_heads, log_total, 0, count)
    late = []
    if number_of == 2:
        late = three_grad(three, 0)
        three = tie(three, far(late))
        late = send(late)
    three, inner_parts, out_parts = sync(three, inner_parts, out_parts)
    early = fold(outer_parts, inner_parts, out_parts)
    three = tie(three, far(early))
    early = send(early)
    if number_of == 2:
        three = attention_backward(joined, grad_mixed, mixed_heads, log_total, count, count, three)
    three, early, late = sync(three, early, late)
    early = fold(early)
    three = tie(three, far(early))
    threes = [three] + [hop(three[:, k * own_rows : (k + 1) * own_rows], k) for k in others]
    early = send(early)
    more = three_grad(three, number_of - 1)
    (threes, fars), early = sync((threes, far(more)), early)
    more = send([dict(p, far=f) for p, f in zip(more, fars)])
    early = fold(early)
    threes[0] = tie(threes[0], far(early))
    early_one, early_two = send(early[:1]), early[1:]
    input_grad = input_back(places, threes, (query_weight, key_weight, value_weight), grad_one, masked)
    home_grad = home(input_grad)
    _, more, early_one = sync((input_grad, layer_out), more, early_one)
    late = fold(late, more) if late else fold(more)
    for p, f in zip(early_two, tie(far(early_two), far(late))):
        p["far"] = f
    late, early_two = send(late), send(early_two)
    while len((early_one + early_two)[0]["order"][0]) > 1:
        early_one, early_two = send(fold(early_one + early_two)), []

    lines = width // number
    _, late, early_two = sync(far(late), late, early_two)
    if len(late[0]["order"][0]) > 1:
        late = fold(late)
        early_one = [dict(p, near=tie(p["near"], far(late))) for p in early_one]
        home_grad = tie(home_grad, far(late))
        late = send(late)
    made, early = final(
        early_one + early_two, places, size, lines, {"outer": (hidden // number, width)},
        {"inner": 0, "out": hidden_share},
    )
    outer_weight_grad = made["outer"]
    early_away = [hop(early[k], k) for k in others]
    input_grad = wide(home_grad)
    late = after(late, input_grad, outer_weight_grad)
    while len(late[0]["order"][0]) > 1:
        late = fold(late)
        early_away = tie(early_away, far(late))
        late = send(late)
    early = [early[0]] + early_away
    inner_weight_grad = absolute([e[:lines, :hidden_share] for e in early], 1)
    out_weight_grad = absolute([e[:lines, hidden_share:] for e in early], 1)
    team_lines, team_hidden = width // teams, hidden // teams
    flat_rows = -(-(6 * team_lines + team_hidden) // CHUNK)
    flat = sum(e[lines : lines + flat_rows, :CHUNK] for e in early).reshape(1, -1)
    six = cut(flat[:, : 6 * team_lines].reshape(6, team_lines), rank, lines, 1)
    inner_bias_grad = cut(
        flat[:, 6 * team_lines : 6 * team_lines + team_hidden], rank, team_hidden // size, 1
    )
    _, late = final(
        after(late, inner_weight_grad, out_weight_grad), places, size, lines, {},
        {f"three{g}": g * 3 * part for g in range(number_of)},
    )
    late = [late[0]] + [hop(late[k], k) for k in others]

    def three_columns(e, k):
        cuts = [
            e[:lines, (g * 3 + k) * part : (g * 3 + k + 1) * part] for g in range(number_of)
        ]
        return jnp.concatenate(cuts, axis=1)

    three_grads = [absolute([three_columns(e, k) for e in late], 1) for k in range(3)]
    biases = sum(e[lines, : 2 * team_lines] for e in late).reshape(2, team_lines)
    biases = cut(biases, rank, lines, 1)
    spots = [biases[0], biases[1], six[2], six[0], six[1], inner_bias_grad[0], six[5], six[3], six[4]]

    return (
        layer_out,
        input_grad,
        three_grads[0],
        spots[0],
        three_grads[1],
        three_grads[2],
        spots[1],
        out_weight_grad,
        spots[2],
        spots[3],
        spots[4],
        inner_weight_grad,
        spots[5],
        outer_weight_grad,
        spots[6],
        spots[7],
        spots[8],
    )


def solution(mesh):
    split = P("dp", "blk", None)
    row = P("dp")
    both = P(BOTH)
    in_specs = (split, row, row, row, row) + (P(),) * 15
    out_specs = (split, split) + (both,) * 15
    return jax.shard_map(
        per_device, mesh=mesh, in_specs=in_specs, out_specs=out_specs, check_vma=False
    )
```

profile of v0, /device:TPU:0, one launch (start us, length us, event | category | flops | bytes accessed | tf_op | source)
XLA Modules:
  0.0 289.3 jit_solution(11641996513756269399)
XLA Ops:
  0.7 5.2 %all-to-all-start = ((bf16[8,64,1024]{2,1,0:T(8,128)(2,1)}), bf16[8,64,1024]{2,1,0:T(8,128)(2,1)}, u32[]{:S(2)}, u32[]{:S(2)}) async-start(bf16[8,64,1024]{2,1,0:T(8,128)(2,1)} %bitcast.79), calls=%async_computation | async-start | bytes 2097152 | tf_op jit(solution)/shard_map/all_to_all | solution.py:930
  5.9 2.6 copy.40.replace_ref
  8.6 2.2 copy.41.cotangent_ref
  10.9 1.7 copy-done.13
  12.6 1.9 masked_rows.1
  14.5 1.0 copy-done.29
  15.5 1.0 copy-done.30
  18.0 3.3 %constant_dynamic-slice_fusion.3 = (bf16[512,1024]{1,0:T(8,128)(2,1)}, bf16[512,1024]{1,0:T(8,128)(2,1)}) fusion(bf16[1024,1024]{1,0:T(8,128)(2,1)} %param.30, s32[]{:T(128)S(6)} %select_n.115, s32[]{:T(128)S(6)} %select_n.114), kind=kLoop, calls=%fused_computation.55 | loop fusion | bytes 4194312 | tf_op jit(solution)/shard_map/dynamic_slice | solution.py:887
  21.4 1.5 bitcast_select_fusion.current_ref.refs_0_
  24.1 1.6 collective-permute-done.refs_1_
  25.7 3.4 %add_convert_fusion.query_ref.key_ref.value_ref = bf16[1024,1536]{1,0:T(8,128)(2,1)S(1)} fusion(f32[1536]{0:T(1024)S(1)} %maximum_convert_fusion, bf16[512,1024]{1,0:T(8,128)(2,1)S(1)} %collective-permute-done.refs_1_, bf16[512,1024]{1,0:T(8,128)(2,1)S(1)} %bitcast_select_fusion.current_ref.refs_0_, bf16[1024,512]{1,0:T(8,128)(2,1)S(1)} %get-tuple-element.307, ...), kind=kOutput, calls=%fused_computation | convolution fusion | flops 3238002688 | bytes 8394752 | tf_op jit(solution)/shard_map/dot_general | solution.py:23
  29.1 1.0 copy-done.15
  30.1 13.9 %attention_forward.1 = (bf16[1024,512]{1,0:T(8,128)(2,1)S(1)}, f32[4,2,1024]{2,1,0:T(2,128)S(1)}) custom-call(bf16[1024,1536]{1,0:T(8,128)(2,1)S(1)} %add_convert_fusion.query_ref.key_ref.value_ref, bf16[1024,1536]{1,0:T(8,128)(2,1)S(1)} %add_convert_fusion.query_ref.key_ref.value_ref, bf16[1024,1536]{1,0:T(8,128)(2,1)S(1)} %add_convert_fusion.query_ref.key_ref.value_ref), custom_call_target="tpu_custom_call" | custom-call | flops 1 | bytes 1 | tf_op jit(solution)/shard_map/attention_forward/pallas_call | solution.py:141
  44.0 1.0 copy-done.1
  46.8 1.0 collective-permute-done.1.refs_1_
  48.6 6.9 %first_half.1 = (f32[512,1024]{1,0:T(8,128)}, bf16[1024,512]{1,0:T(8,128)(2,1)}, bf16[512,1024]{1,0:T(8,128)(2,1)}, f32[512,1024]{1,0:T(8,128)}, f32[512,1]{1,0:T(8,128)}) custom-call(bf16[512,1024]{1,0:T(8,128)(2,1)} %copy-done.4, f32[6,1,1024]{2,1,0:T(1,128)} %convert_element_type.32.bias_ref.gain_ref.shift_ref.outer_bias_ref, ...), custom_call_target="tpu_custom_call" | custom-call | flops 1 | bytes 1 | tf_op jit(solution)/shard_map/first_half/pallas_call | solution.py:262
  55.5 26.0 %feed_forward.1 = (bf16[2048,512]{1,0:T(8,128)(2,1)}, bf16[2048,512]{1,0:T(8,128)(2,1)}, bf16[512,4096]{1,0:T(8,128)(2,1)}, bf16[512,1024]{1,0:T(8,128)(2,1)}, f...) custom-call(s32[2]{0:T(128)} %pad_add_fusion.place_ref, ...), custom_call_target="tpu_custom_call" | custom-call | flops 1 | bytes 1 | tf_op jit(solution)/shard_map/feed_forward/pallas_call | solution.py:346
  82.0 4.1 %all-to-all-start.1 = ((bf16[8,64,1024]{2,1,0:T(8,128)(2,1)}), bf16[8,64,1024]{2,1,0:T(8,128)(2,1)S(1)}, u32[]{:S(2)}, u32[]{:S(2)}) async-start(bf16[8,64,1024]{2,1,0:T(8,128)(2,1)} %bitcast.80), calls=%async_computation.1 | async-start | bytes 2097152 | tf_op jit(solution)/shard_map/all_to_all | solution.py:985
  86.1 25.3 %feed_back.1 = (bf16[512,2048]{1,0:T(8,128)(2,1)}, bf16[512,2048]{1,0:T(8,128)(2,1)}, f32[1,4096]{1,0:T(1,128)}, f32[512,1024]{1,0:T(8,128)}, bf16[512,1024]{1,0...) custom-call(s32[2]{0:T(128)} %pad_add_fusion.place_ref, ...), custom_call_target="tpu_custom_call" | custom-call | flops 1 | bytes 1 | tf_op jit(solution)/shard_map/feed_back/pallas_call | solution.py:452
  112.8 9.6 %weight_grad.5 = (bf16[8,4,80,256]{3,2,1,0:T(8,128)(2,1)}, bf16[8,4,80,256]{3,2,1,0:T(8,128)(2,1)}, bf16[8,4,48,256]{3,2,1,0:T(8,128)(2,1)}, bf16[8,4,48,256]{3,2,1,0:T(8,128)(2,1)}) custom-call(s32[2]{0:T(128)} %pad_add_fusion.place_ref, bf16[2048,512]{1,0:T(8,128)(2,1)} %get-tuple-element.176.refs_0_, bf16[2048,512]{1,0:T(8,128)(2,1)} %copy-done.53, ...), custom_call_target="tpu_custom_call" | custom-call | flops 1 | bytes 1 | tf_op jit(solution)/shard_map/weight_grad/pallas_call | solution.py:671
  122.4 2.1 collective-permute-start.8
  125.0 2.0 collective-permute-start.9
  128.0 1.5 collective-permute-done.6.refs_5_
  129.5 5.4 %weight_grad.6 = (bf16[8,2,64,256]{3,2,1,0:T(8,128)(2,1)}, bf16[8,2,64,256]{3,2,1,0:T(8,128)(2,1)}) custom-call(s32[2]{0:T(128)} %pad_add_fusion.1.place_ref, bf16[1024,512]{1,0:T(8,128)(2,1)} %copy-done.1, bf16[512,512]{1,0:T(8,128)(2,1)} %copy-done.54, bf16[1024,512]{1,0:T(8,128)(2,1)} %copy-done.1, bf16[512,512]{1,0:T(8,128)(2,1)} %collective-permute-done.5.refs_3_, ...), custom_call_target="tpu_custom_call" | custom-call | flops 1 | bytes 1 | tf_op jit(solution)/shard_map/weight_grad/pallas_call | solution.py:671
  135.9 11.3 %weight_grad.7 = (bf16[8,8,48,256]{3,2,1,0:T(8,128)(2,1)}, bf16[8,8,48,256]{3,2,1,0:T(8,128)(2,1)}, bf16[8,9,16,256]{3,2,1,0:T(8,128)(2,1)}, bf16[8,9,16,256]{3,2,1,0:T(8,128)(2,1)}) custom-call(s32[2]{0:T(128)} %pad_add_fusion.place_ref, bf16[1024,512]{1,0:T(8,128)(2,1)} %get-tuple-element.173.refs_0_, bf16[1024,512]{1,0:T(8,128)(2,1)} %copy-done.55, ...), custom_call_target="tpu_custom_call" | custom-call | flops 1 | bytes 1 | tf_op jit(solution)/shard_map/weight_grad/pallas_call | solution.py:671
  147.3 1.0 collective-permute-start.11
  148.3 2.0 collective-permute-start.12
  150.4 1.0 collective-permute-start.13
  152.3 1.4 copy-done.2
  153.7 13.3 %attention_backward.2.refs_2_.refs_3_ = bf16[3,1024,512]{2,1,0:T(8,128)(2,1)S(1)} custom-call(bf16[1024,1536]{1,0:T(8,128)(2,1)} %copy-done, bf16[1024,1536]{1,0:T(8,128)(2,1)} %copy-done, bf16[1024,1536]{1,0:T(8,128)(2,1)} %copy-done, bf16[1024,512]{1,0:T(8,128)(2,1)S(1)} %copy-done.2, f32[4,2,1024]{2,1,0:T(2,128)S(1)} %get-tuple-element.171.log_ref, ...), custom_call_target="tpu_custom_call" | custom-call | flops 1 | bytes 1 | tf_op jit(solution)/shard_map/attention_backward/pallas_call | solution.py:170
  167.1 4.1 %weight_grad.8 = (bf16[8,3,48,256]{3,2,1,0:T(8,128)(2,1)S(1)}, bf16[8,3,48,256]{3,2,1,0:T(8,128)(2,1)S(1)}, bf16[8,4,16,256]{3,2,1,0:T(8,128)(2,1)S(1)}, bf16[8,4,16,256]{3,2,1,0:T(8,128)(2,1)S(1)}) custom-call(s32[2]{0:T(128)S(1)} %copy-done.42, bf16[512,1024]{1,0:T(8,128)(2,1)S(1)} %copy-done.5, bf16[512,1024]{1,0:T(8,128)(2,1)S(1)} %copy-done.16, ...), custom_call_target="tpu_custom_call" | custom-call | flops 1 | bytes 1 | tf_op jit(solution)/shard_map/weight_grad/pallas_call | solution.py:671
  173.7 6.4 %fold.6 = (bf16[4,832,256]{2,1,0:T(8,128)(2,1)}, bf16[4,832,256]{2,1,0:T(8,128)(2,1)}, bf16[4,336,256]{2,1,0:T(8,128)(2,1)}, bf16[4,336,256]{2,1,0:T(8,128)(2,1)}) custom-call(bf16[8,320,256]{2,1,0:T(8,128)(2,1)} %bitcast.70, bf16[8,320,256]{2,1,0:T(8,128)(2,1)} %bitcast.71, bf16[8,320,256]{2,1,0:T(8,128)(2,1)} %copy-done.48, ...), custom_call_target="tpu_custom_call" | custom-call | flops 1 | bytes 1 | tf_op jit(solution)/shard_map/fold/pallas_call | solution.py:761
  180.1 2.0 collective-permute-start.14
  182.2 1.5 collective-permute-start.15
  184.5 1.2 copy-done.3
  185.7 1.0 copy-done.26
  186.8 1.0 copy-done.28
  187.8 13.3 %attention_backward.3.refs_2_.refs_3_.refs_0_ = bf16[3,1024,512]{2,1,0:T(8,128)(2,1)S(1)} custom-call(bf16[1024,1536]{1,0:T(8,128)(2,1)} %copy-done, bf16[1024,1536]{1,0:T(8,128)(2,1)} %copy-done, bf16[1024,1536]{1,0:T(8,128)(2,1)} %copy-done, bf16[1024,512]{1,0:T(8,128)(2,1)S(1)} %copy-done.3, ...), custom_call_target="tpu_custom_call", output_to_operand_aliasing={{}: (7, {})} | custom-call | flops 1 | bytes 1 | tf_op jit(solution)/shard_map/attention_backward/pallas_call | solution.py:170
  201.1 6.7 %collective-permute-done.17.refs_10_.refs_11_ = bf16[8,64,256]{2,1,0:T(8,128)(2,1)S(1)} collective-permute-done((bf16[8,64,256]{2,1,0:T(8,128)(2,1)}, bf16[8,64,256]{2,1,0:T(8,128)(2,1)S(1)}, u32[]{:S(2)}, u32[]{:S(2)}) %collective-permute-start.17) | collective-permute-done | bytes 262176 | tf_op jit(solution)/shard_map/ppermute | solution.py:909
  209.0 1.6 collective-permute-start.19
  211.3 4.7 %weight_grad.9 = (bf16[8,3,48,256]{3,2,1,0:T(8,128)(2,1)S(1)}, bf16[8,3,48,256]{3,2,1,0:T(8,128)(2,1)}, bf16[8,4,16,256]{3,2,1,0:T(8,128)(2,1)S(1)}, bf16[8,4,16,256]{3,2,1,0:T(8,128)(2,1)}) custom-call(s32[2]{0:T(128)S(1)} %copy-done.42, bf16[512,1024]{1,0:T(8,128)(2,1)S(1)} %copy-done.6, bf16[512,1024]{1,0:T(8,128)(2,1)S(1)} %copy-done.17, ...), custom_call_target="tpu_custom_call" | custom-call | flops 1 | bytes 1 | tf_op jit(solution)/shard_map/weight_grad/pallas_call | solution.py:671
  217.5 3.6 %collective-permute-done.20.refs_6_.refs_7_ = bf16[2,336,256]{2,1,0:T(8,128)(2,1)S(1)} collective-permute-done((bf16[2,336,256]{2,1,0:T(8,128)(2,1)S(1)}, bf16[2,336,256]{2,1,0:T(8,128)(2,1)S(1)}, u32[]{:S(2)}, u32[]{:S(2)}) %collective-permute-start.20) | collective-permute-done | bytes 344096 | tf_op jit(solution)/shard_map/ppermute | solution.py:909
  221.7 1.0 collective-permute-start.21
  222.7 1.0 fold.8
  224.4 3.0 %collective-permute-start.23 = (bf16[1,832,256]{2,1,0:T(8,128)(2,1)}, bf16[1,832,256]{2,1,0:T(8,128)(2,1)}, u32[]{:S(2)}, u32[]{:S(2)}) collective-permute-start(bf16[1,832,256]{2,1,0:T(8,128)(2,1)} %get-tuple-element.228), channel_id=1, source_target_pairs={{0,16},{1,17},{2,18},{3,19},{4,20},{5,21},{6,22},{7,23},{8,24},{9,... | collective-permute-start | bytes 1277960 | tf_op jit(solution)/shard_map/ppermute | solution.py:909
  227.4 1.6 collective-permute-start.22
  229.0 5.0 %input_back.1 = bf16[512,1024]{1,0:T(8,128)(2,1)S(1)} custom-call(s32[2]{0:T(128)S(1)} %copy-done.42, f32[512,1024]{1,0:T(8,128)S(1)} %copy-done.24, f32[512,1]{1,0:T(8,128)S(1)} %get-tuple-element.145.masked_ref, bf16[3,1024,512]{2,1,0:T(8,128)(2,1)S(1)} %attention_backward.3.refs_2_.refs_3_.refs_0_, ...), custom_call_target="tpu_custom_call" | custom-call | flops 1 | bytes 1 | tf_op jit(solution)/shard_map/input_back/pallas_call | solution.py:507
  234.0 1.0 copy-done.18
  234.9 4.4 %all-to-all-start.2 = ((bf16[8,64,1024]{2,1,0:T(8,128)(2,1)}), bf16[8,64,1024]{2,1,0:T(8,128)(2,1)}, u32[]{:S(2)}, u32[]{:S(2)}) async-start(bf16[8,64,1024]{2,1,0:T(8,128)(2,1)} %bitcast.57), calls=%async_computation.2 | async-start | bytes 2097152 | tf_op jit(solution)/shard_map/all_to_all | solution.py:985
  239.4 1.6 bitcast_convert_fusion.1
  241.0 1.5 collective-permute-done.22.refs_14_.refs_15_
  242.4 4.2 %collective-permute-done.23.refs_1_ = bf16[1,832,256]{2,1,0:T(8,128)(2,1)} collective-permute-done((bf16[1,832,256]{2,1,0:T(8,128)(2,1)}, bf16[1,832,256]{2,1,0:T(8,128)(2,1)}, u32[]{:S(2)}, u32[]{:S(2)}) %collective-permute-start.23) | collective-permute-done | bytes 426016 | tf_op jit(solution)/shard_map/ppermute | solution.py:909
  246.7 2.3 fold.9
  250.4 3.4 %collective-permute-start.26 = (bf16[1,336,256]{2,1,0:T(8,128)(2,1)S(1)}, bf16[1,336,256]{2,1,0:T(8,128)(2,1)S(1)}, u32[]{:S(2)}, u32[]{:S(2)}) collective-permute-start(bf16[1,336,256]{2,1,0:T(8,128)(2,1)S(1)} %copy-done.47), channel_id=1, source_target_pairs={{0,16},{1,17},{2,18},{3,19},{4,20},{5,21},{6,22},{7,23},{8,24},{9,... | collective-permute-start | bytes 516104 | tf_op jit(solution)/shard_map/ppermute | solution.py:909
  253.8 5.6 %collective-permute-done.26.refs_3_ = bf16[1,336,256]{2,1,0:T(8,128)(2,1)S(1)} collective-permute-done((bf16[1,336,256]{2,1,0:T(8,128)(2,1)S(1)}, bf16[1,336,256]{2,1,0:T(8,128)(2,1)S(1)}, u32[]{:S(2)}, u32[]{:S(2)}) %collective-permute-start.26) | collective-permute-done | bytes 172064 | tf_op jit(solution)/shard_map/ppermute | solution.py:909
  259.5 2.9 %collective-permute-done.24.refs_2_.refs_3_ = bf16[4,288,256]{2,1,0:T(8,128)(2,1)S(1)} collective-permute-done((bf16[4,288,256]{2,1,0:T(8,128)(2,1)S(1)}, bf16[4,288,256]{2,1,0:T(8,128)(2,1)S(1)}, u32[]{:S(2)}, u32[]{:S(2)}) %collective-permute-start.24) | collective-permute-done | bytes 589856 | tf_op jit(solution)/shard_map/ppermute | solution.py:909
  262.7 1.9 final.2
  265.4 1.0 collective-permute-start.28
  266.4 2.8 bitcast_convert_fusion
  269.1 1.8 collective-permute-done.28.refs_6_.refs_7_
  271.4 1.9 collective-permute-start.29
  273.4 1.0 collective-permute-start.30
  276.7 7.7 %collective-permute-done.30.refs_3_ = bf16[1,128,256]{2,1,0:T(8,128)(2,1)S(1)} collective-permute-done((bf16[1,128,256]{2,1,0:T(8,128)(2,1)S(1)}, bf16[1,128,256]{2,1,0:T(8,128)(2,1)S(1)}, u32[]{:S(2)}, u32[]{:S(2)}) %collective-permute-start.30) | collective-permute-done | bytes 65568 | tf_op jit(solution)/shard_map/ppermute | solution.py:909
  285.6 1.0 collective-permute-done.32
  (217 shorter events, 28.2 us)
Async XLA Ops:
  0.7 20.7 %all-to-all-start = ((bf16[8,64,1024]{2,1,0:T(8,128)(2,1)}), bf16[8,64,1024]{2,1,0:T(8,128)(2,1)}, u32[]{:S(2)}, u32[]{:S(2)}) async-start(bf16[8,64,1024]{2,1,0:T(8,128)(2,1)} %bitcast.79), calls=%async_computation | async-start | bytes 2097152 | tf_op jit(solution)/shard_map/all_to_all | solution.py:930
  12.6 4.6 %copy-start.57 = (bf16[4096]{0:T(1024)(128)(2,1)S(1)}, bf16[4096]{0:T(1024)(128)(2,1)}, u32[]{:S(2)}) copy-start(bf16[4096]{0:T(1024)(128)(2,1)} %param.35) | copy-start | bytes 24580
  18.0 5.6 %copy-start.11 = (bf16[1024,1024]{1,0:T(8,128)(2,1)S(1)}, bf16[1024,1024]{1,0:T(8,128)(2,1)}, u32[]{:S(2)}) copy-start(bf16[1024,1024]{1,0:T(8,128)(2,1)} %refs_5_.1) | copy-start | bytes 6291460
  22.9 2.8 collective-permute-start
  30.1 13.9 %copy-start = (bf16[1024,1536]{1,0:T(8,128)(2,1)}, bf16[1024,1536]{1,0:T(8,128)(2,1)S(1)}, u32[]{:S(2)}) copy-start(bf16[1024,1536]{1,0:T(8,128)(2,1)S(1)} %add_convert_fusion.query_ref.key_ref.value_ref) | copy-start | bytes 9437188
  45.9 1.9 collective-permute-start.1
  81.4 30.0 %collective-permute-start.3 = (bf16[2048,512]{1,0:T(8,128)(2,1)}, bf16[2048,512]{1,0:T(8,128)(2,1)S(1)}, u32[]{:S(2)}, u32[]{:S(2)}) collective-permute-start(bf16[2048,512]{1,0:T(8,128)(2,1)} %get-tuple-element.168), channel_id=1, source_target_pairs={{0,1},{1,0},{2,3},{3,2},{4,5},{5,4},{6,7},{7,6},{8,9},{9,8},{10,11... | collective-permute-start | bytes 6291464 | tf_op jit(solution)/shard_map/ppermute | solution.py:884
  81.9 29.6 %collective-permute-start.2 = (bf16[512,1024]{1,0:T(8,128)(2,1)}, bf16[512,1024]{1,0:T(8,128)(2,1)}, u32[]{:S(2)}, u32[]{:S(2)}) collective-permute-start(bf16[512,1024]{1,0:T(8,128)(2,1)} %get-tuple-element.178.grad_low_ref.refs_2_), channel_id=1, source_target_pairs={{0,1},{1,0},{2,3},{3,2},{4,5},{5,4},{6,7},{7,6},{8,9},{9,8},{10,11... | collective-permute-start | bytes 3145736 | tf_op jit(solution)/shard_map/ppermute | solution.py:884
  82.0 29.4 %all-to-all-start.1 = ((bf16[8,64,1024]{2,1,0:T(8,128)(2,1)}), bf16[8,64,1024]{2,1,0:T(8,128)(2,1)S(1)}, u32[]{:S(2)}, u32[]{:S(2)}) async-start(bf16[8,64,1024]{2,1,0:T(8,128)(2,1)} %bitcast.80), calls=%async_computation.1 | async-start | bytes 2097152 | tf_op jit(solution)/shard_map/all_to_all | solution.py:985
  111.4 11.0 %copy-start.49 = (bf16[8,64,1024]{2,1,0:T(8,128)(2,1)}, bf16[8,64,1024]{2,1,0:T(8,128)(2,1)S(1)}, u32[]{:S(2)}) copy-start(bf16[8,64,1024]{2,1,0:T(8,128)(2,1)S(1)} %all-to-all-done.1) | copy-start | bytes 3145732
  111.5 13.0 %copy-start.56 = (bf16[512,512]{1,0:T(8,128)(2,1)S(1)}, bf16[512,512]{1,0:T(8,128)(2,1)}, u32[]{:S(2)}) copy-start(bf16[512,512]{1,0:T(8,128)(2,1)} %get-tuple-element.275) | copy-start | bytes 1572868
  111.5 23.5 %collective-permute-start.7 = (bf16[512,2048]{1,0:T(8,128)(2,1)}, bf16[512,2048]{1,0:T(8,128)(2,1)}, u32[]{:S(2)}, u32[]{:S(2)}) collective-permute-start(bf16[512,2048]{1,0:T(8,128)(2,1)} %get-tuple-element.186), channel_id=1, source_target_pairs={{0,1},{1,0},{2,3},{3,2},{4,5},{5,4},{6,7},{7,6},{8,9},{9,8},{10,11... | collective-permute-start | bytes 6291464 | tf_op jit(solution)/shard_map/ppermute | solution.py:884
  122.4 24.8 %collective-permute-start.8 = (bf16[8,320,256]{2,1,0:T(8,128)(2,1)}, bf16[8,320,256]{2,1,0:T(8,128)(2,1)S(1)}, u32[]{:S(2)}, u32[]{:S(2)}) collective-permute-start(bf16[8,320,256]{2,1,0:T(8,128)(2,1)} %bitcast.84), channel_id=1, source_target_pairs={{0,2},{1,5},{2,0},{3,7},{4,6},{5,1},{6,4},{7,3},{8,10},{9,13},{10,... | collective-permute-start | bytes 3932168 | tf_op jit(solution)/shard_map/ppermute | solution.py:909
  124.5 2.8 collective-permute-start.5
  124.5 10.4 %collective-permute-start.4 = (bf16[1024,512]{1,0:T(8,128)(2,1)}, bf16[1024,512]{1,0:T(8,128)(2,1)S(1)}, u32[]{:S(2)}, u32[]{:S(2)}) collective-permute-start(bf16[1024,512]{1,0:T(8,128)(2,1)} %get-tuple-element.173.refs_0_), channel_id=1, source_target_pairs={{0,1},{1,0},{2,3},{3,2},{4,5},{5,4},{6,7},{7,6},{8,9},{9,8},{10,11... | collective-permute-start | bytes 3145736 | tf_op jit(solution)/shard_map/ppermute | solution.py:884
  125.0 22.2 %collective-permute-start.9 = (bf16[8,192,256]{2,1,0:T(8,128)(2,1)}, bf16[8,192,256]{2,1,0:T(8,128)(2,1)S(1)}, u32[]{:S(2)}, u32[]{:S(2)}) collective-permute-start(bf16[8,192,256]{2,1,0:T(8,128)(2,1)} %bitcast.85), channel_id=1, source_target_pairs={{0,8},{1,9},{2,10},{3,11},{4,12},{5,13},{6,14},{7,15},{8,0},{9,1},... | collective-permute-start | bytes 2359304 | tf_op jit(solution)/shard_map/ppermute | solution.py:909
  127.3 2.3 collective-permute-start.6
  135.9 14.4 %copy-start.67 = (bf16[512,512]{1,0:T(8,128)(2,1)S(1)}, bf16[512,512]{1,0:T(8,128)(2,1)}, u32[]{:S(2)}) copy-start(bf16[512,512]{1,0:T(8,128)(2,1)} %get-tuple-element.195) | copy-start | bytes 1572868
  135.9 16.3 %copy-start.25 = (bf16[512,512]{1,0:T(8,128)(2,1)S(1)}, bf16[512,512]{1,0:T(8,128)(2,1)}, u32[]{:S(2)}) copy-start(bf16[512,512]{1,0:T(8,128)(2,1)} %get-tuple-element.194.refs_0_) | copy-start | bytes 1572868
  147.3 5.0 %copy-start.51 = (bf16[8,192,256]{2,1,0:T(8,128)(2,1)}, bf16[8,192,256]{2,1,0:T(8,128)(2,1)S(1)}, u32[]{:S(2)}) copy-start(bf16[8,192,256]{2,1,0:T(8,128)(2,1)S(1)} %collective-permute-done.9.refs_14_.refs_15_) | copy-start | bytes 2359300
  147.3 5.0 %copy-start.48 = (bf16[8,320,256]{2,1,0:T(8,128)(2,1)}, bf16[8,320,256]{2,1,0:T(8,128)(2,1)S(1)}, u32[]{:S(2)}) copy-start(bf16[8,320,256]{2,1,0:T(8,128)(2,1)S(1)} %collective-permute-done.8.refs_2_.refs_3_) | copy-start | bytes 3932164
  147.3 26.4 %collective-permute-start.11 = (bf16[8,384,256]{2,1,0:T(8,128)(2,1)}, bf16[8,384,256]{2,1,0:T(8,128)(2,1)}, u32[]{:S(2)}, u32[]{:S(2)}) collective-permute-start(bf16[8,384,256]{2,1,0:T(8,128)(2,1)} %bitcast.83), channel_id=1, source_target_pairs={{0,2},{1,5},{2,0},{3,7},{4,6},{5,1},{6,4},{7,3},{8,10},{9,13},{10,... | collective-permute-start | bytes 4718600 | tf_op jit(solution)/shard_map/ppermute | solution.py:909
  148.3 25.4 %collective-permute-start.12 = (bf16[8,144,256]{2,1,0:T(8,128)(2,1)}, bf16[8,144,256]{2,1,0:T(8,128)(2,1)}, u32[]{:S(2)}, u32[]{:S(2)}) collective-permute-start(bf16[8,144,256]{2,1,0:T(8,128)(2,1)} %bitcast.86), channel_id=1, source_target_pairs={{0,8},{1,9},{2,10},{3,11},{4,12},{5,13},{6,14},{7,15},{8,0},{9,1},... | collective-permute-start | bytes 1769480 | tf_op jit(solution)/shard_map/ppermute | solution.py:909
  150.3 1.9 collective-permute-start.10
  150.4 23.3 %collective-permute-start.13 = (bf16[8,128,256]{2,1,0:T(8,128)(2,1)}, bf16[8,128,256]{2,1,0:T(8,128)(2,1)}, u32[]{:S(2)}, u32[]{:S(2)}) collective-permute-start(bf16[8,128,256]{2,1,0:T(8,128)(2,1)} %bitcast.87), channel_id=1, source_target_pairs={{0,2},{1,5},{2,0},{3,7},{4,6},{5,1},{6,4},{7,3},{8,10},{9,13},{10,... | collective-permute-start | bytes 1572872 | tf_op jit(solution)/shard_map/ppermute | solution.py:909
  152.2 14.8 %copy-start.27 = (bf16[512,512]{1,0:T(8,128)(2,1)}, bf16[512,512]{1,0:T(8,128)(2,1)S(1)}, u32[]{:S(2)}) copy-start(bf16[512,512]{1,0:T(8,128)(2,1)S(1)} %collective-permute-done.10.refs_1_) | copy-start | bytes 1572868
  153.7 13.4 %copy-start.5 = (bf16[512,1024]{1,0:T(8,128)(2,1)S(1)}, bf16[512,1024]{1,0:T(8,128)(2,1)}, u32[]{:S(2)}) copy-start(bf16[512,1024]{1,0:T(8,128)(2,1)} %copy-done.4) | copy-start | bytes 3145732
  153.7 13.4 %copy-start.16 = (bf16[512,1024]{1,0:T(8,128)(2,1)S(1)}, bf16[512,1024]{1,0:T(8,128)(2,1)}, u32[]{:S(2)}) copy-start(bf16[512,1024]{1,0:T(8,128)(2,1)} %copy-done.15) | copy-start | bytes 3145732
  153.7 13.4 %copy-start.42 = (s32[2]{0:T(128)S(1)}, s32[2]{0:T(128)}, u32[]{:S(2)}) copy-start(s32[2]{0:T(128)} %pad_add_fusion.place_ref) | copy-start | bytes 28
  180.1 27.7 %collective-permute-start.14 = (bf16[4,832,256]{2,1,0:T(8,128)(2,1)}, bf16[4,832,256]{2,1,0:T(8,128)(2,1)S(1)}, u32[]{:S(2)}, u32[]{:S(2)}) collective-permute-start(bf16[4,832,256]{2,1,0:T(8,128)(2,1)} %get-tuple-element.210), channel_id=1, source_target_pairs={{0,8},{1,3},{2,10},{3,1},{4,12},{5,7},{6,14},{7,5},{8,0},{9,11},{1... | collective-permute-start | bytes 5111816 | tf_op jit(solution)/shard_map/ppermute | solution.py:909
  182.2 25.7 %collective-permute-start.15 = (bf16[4,336,256]{2,1,0:T(8,128)(2,1)}, bf16[4,336,256]{2,1,0:T(8,128)(2,1)S(1)}, u32[]{:S(2)}, u32[]{:S(2)}) collective-permute-start(bf16[4,336,256]{2,1,0:T(8,128)(2,1)} %get-tuple-element.211), channel_id=1, source_target_pairs={{0,4},{1,5},{2,6},{3,7},{4,0},{5,1},{6,2},{7,3},{8,12},{9,13},{10,... | collective-permute-start | bytes 2064392 | tf_op jit(solution)/shard_map/ppermute | solution.py:909
  183.7 24.2 %collective-permute-start.16 = (bf16[8,144,256]{2,1,0:T(8,128)(2,1)}, bf16[8,144,256]{2,1,0:T(8,128)(2,1)S(1)}, u32[]{:S(2)}, u32[]{:S(2)}) collective-permute-start(bf16[8,144,256]{2,1,0:T(8,128)(2,1)} %bitcast.66), channel_id=1, source_target_pairs={{0,2},{1,5},{2,0},{3,7},{4,6},{5,1},{6,4},{7,3},{8,10},{9,13},{10,... | collective-permute-start | bytes 1769480 | tf_op jit(solution)/shard_map/ppermute | solution.py:909
  184.2 23.6 %collective-permute-start.17 = (bf16[8,64,256]{2,1,0:T(8,128)(2,1)}, bf16[8,64,256]{2,1,0:T(8,128)(2,1)S(1)}, u32[]{:S(2)}, u32[]{:S(2)}) collective-permute-start(bf16[8,64,256]{2,1,0:T(8,128)(2,1)} %bitcast.67), channel_id=1, source_target_pairs={{0,8},{1,9},{2,10},{3,11},{4,12},{5,13},{6,14},{7,15},{8,0},{9,1},... | collective-permute-start | bytes 786440 | tf_op jit(solution)/shard_map/ppermute | solution.py:909
  187.8 20.1 %copy-start.14 = (bf16[4,832,256]{2,1,0:T(8,128)(2,1)S(1)}, bf16[4,832,256]{2,1,0:T(8,128)(2,1)}, u32[]{:S(2)}) copy-start(bf16[4,832,256]{2,1,0:T(8,128)(2,1)} %get-tuple-element.214.refs_0_.refs_1_) | copy-start | bytes 5111812
  187.8 20.1 %copy-start.19 = (bf16[4,336,256]{2,1,0:T(8,128)(2,1)S(1)}, bf16[4,336,256]{2,1,0:T(8,128)(2,1)}, u32[]{:S(2)}) copy-start(bf16[4,336,256]{2,1,0:T(8,128)(2,1)} %get-tuple-element.216.refs_4_.refs_5_) | copy-start | bytes 2064388
  208.9 12.8 %collective-permute-start.18 = (bf16[3,512,512]{2,1,0:T(8,128)(2,1)S(1)}, bf16[3,512,512]{2,1,0:T(8,128)(2,1)S(1)}, u32[]{:S(2)}, u32[]{:S(2)}) collective-permute-start(bf16[3,512,512]{2,1,0:T(8,128)(2,1)S(1)} %slice.103), channel_id=1, source_target_pairs={{0,1},{1,0},{2,3},{3,2},{4,5},{5,4},{6,7},{7,6},{8,9},{9,8},{10,11... | collective-permute-start | bytes 4718600 | tf_op jit(solution)/shard_map/ppermute | solution.py:884
  209.0 12.8 %collective-permute-start.19 = (bf16[2,832,256]{2,1,0:T(8,128)(2,1)S(1)}, bf16[2,832,256]{2,1,0:T(8,128)(2,1)S(1)}, u32[]{:S(2)}, u32[]{:S(2)}) collective-permute-start(bf16[2,832,256]{2,1,0:T(8,128)(2,1)S(1)} %get-tuple-element.218), channel_id=1, source_target_pairs={{0,4},{1,9},{2,6},{3,11},{4,0},{5,13},{6,2},{7,15},{8,12},{9,1},{1... | collective-permute-start | bytes 2555912 | tf_op jit(solution)/shard_map/ppermute | solution.py:909
  210.5 10.6 %collective-permute-start.20 = (bf16[2,336,256]{2,1,0:T(8,128)(2,1)S(1)}, bf16[2,336,256]{2,1,0:T(8,128)(2,1)S(1)}, u32[]{:S(2)}, u32[]{:S(2)}) collective-permute-start(bf16[2,336,256]{2,1,0:T(8,128)(2,1)S(1)} %get-tuple-element.219), channel_id=1, source_target_pairs={{0,2},{1,3},{2,0},{3,1},{4,6},{5,7},{6,4},{7,5},{8,10},{9,11},{10,... | collective-permute-start | bytes 1032200 | tf_op jit(solution)/shard_map/ppermute | solution.py:909
  211.3 17.7 %copy-start.12 = (bf16[1024,1024]{1,0:T(8,128)(2,1)S(1)}, bf16[1024,1024]{1,0:T(8,128)(2,1)}, u32[]{:S(2)}) copy-start(bf16[1024,1024]{1,0:T(8,128)(2,1)} %refs_5_.1) | copy-start | bytes 6291460
  211.3 17.7 %copy-start.24 = (f32[512,1024]{1,0:T(8,128)S(1)}, f32[512,1024]{1,0:T(8,128)}, u32[]{:S(2)}) copy-start(f32[512,1024]{1,0:T(8,128)} %get-tuple-element.170.grad_ref) | copy-start | bytes 6291460
  221.7 24.9 %collective-permute-start.21 = (bf16[8,144,256]{2,1,0:T(8,128)(2,1)}, bf16[8,144,256]{2,1,0:T(8,128)(2,1)}, u32[]{:S(2)}, u32[]{:S(2)}) collective-permute-start(bf16[8,144,256]{2,1,0:T(8,128)(2,1)} %bitcast.20), channel_id=1, source_target_pairs={{0,2},{1,5},{2,0},{3,7},{4,6},{5,1},{6,4},{7,3},{8,10},{9,13},{10,... | collective-permute-start | bytes 1769480 | tf_op jit(solution)/shard_map/ppermute | solution.py:909
  222.7 6.3 %copy-start.8 = (bf16[1024,1024]{1,0:T(8,128)(2,1)S(1)}, bf16[1024,1024]{1,0:T(8,128)(2,1)}, u32[]{:S(2)}) copy-start(bf16[1024,1024]{1,0:T(8,128)(2,1)} %refs_7_.1) | copy-start | bytes 6291460
  222.7 6.3 %copy-start.10 = (bf16[1024,1024]{1,0:T(8,128)(2,1)S(1)}, bf16[1024,1024]{1,0:T(8,128)(2,1)}, u32[]{:S(2)}) copy-start(bf16[1024,1024]{1,0:T(8,128)(2,1)} %refs_6_.1) | copy-start | bytes 6291460
  224.4 9.6 %copy-start.40 = (bf16[1,336,256]{2,1,0:T(8,128)(2,1)}, bf16[1,336,256]{2,1,0:T(8,128)(2,1)S(1)}, u32[]{:S(2)}) copy-start(bf16[1,336,256]{2,1,0:T(8,128)(2,1)S(1)} %get-tuple-element.256.refs_2_) | copy-start | bytes 516100
  224.4 9.6 %copy-start.46 = (bf16[1,336,256]{2,1,0:T(8,128)(2,1)}, bf16[1,336,256]{2,1,0:T(8,128)(2,1)S(1)}, u32[]{:S(2)}) copy-start(bf16[1,336,256]{2,1,0:T(8,128)(2,1)S(1)} %get-tuple-element.245) | copy-start | bytes 516100
  224.4 22.3 %collective-permute-start.23 = (bf16[1,832,256]{2,1,0:T(8,128)(2,1)}, bf16[1,832,256]{2,1,0:T(8,128)(2,1)}, u32[]{:S(2)}, u32[]{:S(2)}) collective-permute-start(bf16[1,832,256]{2,1,0:T(8,128)(2,1)} %get-tuple-element.228), channel_id=1, source_target_pairs={{0,16},{1,17},{2,18},{3,19},{4,20},{5,21},{6,22},{7,23},{8,24},{9,... | collective-permute-start | bytes 1277960 | tf_op jit(solution)/shard_map/ppermute | solution.py:909
  227.4 15.0 %collective-permute-start.22 = (bf16[8,64,256]{2,1,0:T(8,128)(2,1)}, bf16[8,64,256]{2,1,0:T(8,128)(2,1)}, u32[]{:S(2)}, u32[]{:S(2)}) collective-permute-start(bf16[8,64,256]{2,1,0:T(8,128)(2,1)} %bitcast.21), channel_id=1, source_target_pairs={{0,8},{1,9},{2,10},{3,11},{4,12},{5,13},{6,14},{7,15},{8,0},{9,1},... | collective-permute-start | bytes 786440 | tf_op jit(solution)/shard_map/ppermute | solution.py:909
  234.9 31.4 %all-to-all-start.2 = ((bf16[8,64,1024]{2,1,0:T(8,128)(2,1)}), bf16[8,64,1024]{2,1,0:T(8,128)(2,1)}, u32[]{:S(2)}, u32[]{:S(2)}) async-start(bf16[8,64,1024]{2,1,0:T(8,128)(2,1)} %bitcast.57), calls=%async_computation.2 | async-start | bytes 2097152 | tf_op jit(solution)/shard_map/all_to_all | solution.py:985
  239.3 7.3 %copy-start.21 = (bf16[8,144,256]{2,1,0:T(8,128)(2,1)S(1)}, bf16[8,144,256]{2,1,0:T(8,128)(2,1)}, u32[]{:S(2)}) copy-start(bf16[8,144,256]{2,1,0:T(8,128)(2,1)} %copy-done.20) | copy-start | bytes 1769476
  239.4 7.3 %copy-start.23 = (bf16[8,3,48,256]{3,2,1,0:T(8,128)(2,1)S(1)}, bf16[8,3,48,256]{3,2,1,0:T(8,128)(2,1)}, u32[]{:S(2)}) copy-start(bf16[8,3,48,256]{3,2,1,0:T(8,128)(2,1)} %copy-done.22) | copy-start | bytes 1769476
  239.4 7.3 %copy-start.33 = (bf16[8,4,16,256]{3,2,1,0:T(8,128)(2,1)S(1)}, bf16[8,4,16,256]{3,2,1,0:T(8,128)(2,1)}, u32[]{:S(2)}) copy-start(bf16[8,4,16,256]{3,2,1,0:T(8,128)(2,1)} %copy-done.32) | copy-start | bytes 786436
  239.4 7.3 %copy-start.35 = (bf16[8,64,256]{2,1,0:T(8,128)(2,1)S(1)}, bf16[8,64,256]{2,1,0:T(8,128)(2,1)}, u32[]{:S(2)}) copy-start(bf16[8,64,256]{2,1,0:T(8,128)(2,1)} %copy-done.34) | copy-start | bytes 786436
  239.4 7.3 %copy-start.37 = (bf16[8,4,16,256]{3,2,1,0:T(8,128)(2,1)S(1)}, bf16[8,4,16,256]{3,2,1,0:T(8,128)(2,1)}, u32[]{:S(2)}) copy-start(bf16[8,4,16,256]{3,2,1,0:T(8,128)(2,1)} %copy-done.36) | copy-start | bytes 786436
  249.0 13.6 %copy-start.39 = (bf16[1,832,256]{2,1,0:T(8,128)(2,1)S(1)}, bf16[1,832,256]{2,1,0:T(8,128)(2,1)}, u32[]{:S(2)}) copy-start(bf16[1,832,256]{2,1,0:T(8,128)(2,1)} %copy-done.38) | copy-start | bytes 1277956
  249.0 13.6 %copy-start.41 = (bf16[1,336,256]{2,1,0:T(8,128)(2,1)S(1)}, bf16[1,336,256]{2,1,0:T(8,128)(2,1)}, u32[]{:S(2)}) copy-start(bf16[1,336,256]{2,1,0:T(8,128)(2,1)} %copy-done.40) | copy-start | bytes 516100
  249.1 13.4 %collective-permute-start.24 = (bf16[4,288,256]{2,1,0:T(8,128)(2,1)S(1)}, bf16[4,288,256]{2,1,0:T(8,128)(2,1)S(1)}, u32[]{:S(2)}, u32[]{:S(2)}) collective-permute-start(bf16[4,288,256]{2,1,0:T(8,128)(2,1)S(1)} %get-tuple-element.243), channel_id=1, source_target_pairs={{0,8},{1,3},{2,10},{3,1},{4,12},{5,7},{6,14},{7,5},{8,0},{9,11},{1... | collective-permute-start | bytes 1769480 | tf_op jit(solution)/shard_map/ppermute | solution.py:909
  249.8 9.7 %collective-permute-start.25 = (bf16[4,128,256]{2,1,0:T(8,128)(2,1)S(1)}, bf16[4,128,256]{2,1,0:T(8,128)(2,1)S(1)}, u32[]{:S(2)}, u32[]{:S(2)}) collective-permute-start(bf16[4,128,256]{2,1,0:T(8,128)(2,1)S(1)} %get-tuple-element.244), channel_id=1, source_target_pairs={{0,4},{1,5},{2,6},{3,7},{4,0},{5,1},{6,2},{7,3},{8,12},{9,13},{10,... | collective-permute-start | bytes 786440 | tf_op jit(solution)/shard_map/ppermute | solution.py:909
  250.4 9.0 %collective-permute-start.26 = (bf16[1,336,256]{2,1,0:T(8,128)(2,1)S(1)}, bf16[1,336,256]{2,1,0:T(8,128)(2,1)S(1)}, u32[]{:S(2)}, u32[]{:S(2)}) collective-permute-start(bf16[1,336,256]{2,1,0:T(8,128)(2,1)S(1)} %copy-done.47), channel_id=1, source_target_pairs={{0,16},{1,17},{2,18},{3,19},{4,20},{5,21},{6,22},{7,23},{8,24},{9,... | collective-permute-start | bytes 516104 | tf_op jit(solution)/shard_map/ppermute | solution.py:909
  264.6 9.8 %collective-permute-start.31 = (f32[40,2560]{1,0:T(8,128)S(1)}, f32[40,2560]{1,0:T(8,128)S(1)}, u32[]{:S(2)}, u32[]{:S(2)}) collective-permute-start(f32[40,2560]{1,0:T(8,128)S(1)} %get-tuple-element.266), channel_id=1, source_target_pairs={{0,1},{1,0},{2,3},{3,2},{4,5},{5,4},{6,7},{7,6},{8,9},{9,8},{10,11... | collective-permute-start | bytes 1228808 | tf_op jit(solution)/shard_map/ppermute | solution.py:884
  264.6 6.7 %collective-permute-start.27 = (bf16[2,288,256]{2,1,0:T(8,128)(2,1)S(1)}, bf16[2,288,256]{2,1,0:T(8,128)(2,1)S(1)}, u32[]{:S(2)}, u32[]{:S(2)}) collective-permute-start(bf16[2,288,256]{2,1,0:T(8,128)(2,1)S(1)} %get-tuple-element.249), channel_id=1, source_target_pairs={{0,4},{1,9},{2,6},{3,11},{4,0},{5,13},{6,2},{7,15},{8,12},{9,1},{1... | collective-permute-start | bytes 884744 | tf_op jit(solution)/shard_map/ppermute | solution.py:909
  265.4 5.6 %collective-permute-start.28 = (bf16[2,128,256]{2,1,0:T(8,128)(2,1)S(1)}, bf16[2,128,256]{2,1,0:T(8,128)(2,1)S(1)}, u32[]{:S(2)}, u32[]{:S(2)}) collective-permute-start(bf16[2,128,256]{2,1,0:T(8,128)(2,1)S(1)} %get-tuple-element.250), channel_id=1, source_target_pairs={{0,2},{1,3},{2,0},{3,1},{4,6},{5,7},{6,4},{7,5},{8,10},{9,11},{10,... | collective-permute-start | bytes 393224 | tf_op jit(solution)/shard_map/ppermute | solution.py:909
  271.4 13.0 %collective-permute-start.29 = (bf16[1,288,256]{2,1,0:T(8,128)(2,1)S(1)}, bf16[1,288,256]{2,1,0:T(8,128)(2,1)S(1)}, u32[]{:S(2)}, u32[]{:S(2)}) collective-permute-start(bf16[1,288,256]{2,1,0:T(8,128)(2,1)S(1)} %get-tuple-element.263), channel_id=1, source_target_pairs={{0,16},{1,17},{2,18},{3,19},{4,20},{5,21},{6,22},{7,23},{8,24},{9,... | collective-permute-start | bytes 442376 | tf_op jit(solution)/shard_map/ppermute | solution.py:909
  273.4 11.0 %collective-permute-start.30 = (bf16[1,128,256]{2,1,0:T(8,128)(2,1)S(1)}, bf16[1,128,256]{2,1,0:T(8,128)(2,1)S(1)}, u32[]{:S(2)}, u32[]{:S(2)}) collective-permute-start(bf16[1,128,256]{2,1,0:T(8,128)(2,1)S(1)} %get-tuple-element.264), channel_id=1, source_target_pairs={{0,16},{1,17},{2,18},{3,19},{4,20},{5,21},{6,22},{7,23},{8,24},{9,... | collective-permute-start | bytes 196616 | tf_op jit(solution)/shard_map/ppermute | solution.py:909
  285.0 1.6 collective-permute-start.32
  (40 other events, 79.9 us)
where the time goes:
time: 290 us; the launch traced here: 289 us
  Pallas kernels  154 us (53%)
  starting transfers between devices  46.3 us (16%)
  waiting for transfers between devices  41.7 us (14%)
  local copies, waits for them, and re-layouts  31.2 us (11%)
  other arithmetic  11.5 us (4%)
  matrix products  3.41 us (1%)
    ppermute x21, waiting for transfers between devices, send(): lax.ppermute(p['far'], BOTH, [(i, i ^ size << p['order'][i % size % 2][0]...  35.4 us
    pallas_call x5, Pallas kernels, weight_grad(): pl.pallas_call(functools.partial(weight_kernel, [len(m) for m in lefts],...  35.1 us
    ppermute x21, starting transfers between devices, send(): lax.ppermute(p['far'], BOTH, [(i, i ^ size << p['order'][i % size % 2][0]...  29.7 us
    pallas_call x2, Pallas kernels, attention_backward(): pl.pallas_call(functools.partial(backward_kernel, members), grid=(count,...  26.7 us
    pallas_call x1, Pallas kernels, feed_forward(): pl.pallas_call(functools.partial(feed_kernel, size, hidden // number), gr...  26 us
    pallas_call x1, Pallas kernels, feed_back(): pl.pallas_call(functools.partial(feed_back_kernel, size, steps, share), g...  25.3 us
    unnamed x144, local copies, waits for them, and re-layouts  23.9 us
    pallas_call x1, Pallas kernels, attention_forward(): pl.pallas_call(forward_kernel, grid=(pairs, rows // tile), in_specs=[line...  13.9 us
  transfers between devices with their start and end apart: 36, of which 19 were waited for; matrix products, arithmetic and copies ran while one was open for 6% of the time, Pallas kernels for 34%

commit v1 on v0

--- a/solution.py
+++ b/solution.py
@@ -56,7 +56,7 @@
     return inner * below, below + inner * bell * (1.0 / math.sqrt(2.0 * math.pi))
 
 
-def params(mib=40):
+def params(mib=36):
     return pltpu.CompilerParams(vmem_limit_bytes=mib << 20)
 
 
@@ -147,7 +147,7 @@
             jax.ShapeDtypeStruct((rows, share), LOW),
             jax.ShapeDtypeStruct((pairs, 2, rows), FULL),
         ],
-        compiler_params=params(48),
+        compiler_params=params(40),
         cost_estimate=CHEAP,
         name="attention_forward",
     )(joined, joined, joined)
@@ -183,7 +183,7 @@
         out_shape=jax.ShapeDtypeStruct((3, rows, share), LOW),
         input_output_aliases={5 + members: 0} if more else {},
         scratch_shapes=[pltpu.VMEM((rows, 2 * HEAD), FULL)] * 2,
-        compiler_params=params(48),
+        compiler_params=params(40),
         cost_estimate=CHEAP,
         name="attention_backward",
     )(joined, joined, joined, mixed, log_total, *grad_mixed, *more)
@@ -256,7 +256,7 @@
 
 def first_half(current, mixed, weights, small):
     rows, width = current.shape
-    tile = 128
+    tile = 256
     pieces = len(mixed)
     line = pl.BlockSpec((tile, width), lambda i: (i, 0))
     return pl.pallas_call(
@@ -290,7 +290,7 @@
     outer_bias_ref, gain_ref, shift_ref, *refs,
 ):
     actives = refs[:size]
-    slope_ref, result_ref, grad_ref, grad_low_ref, sums_ref, acc, flip = refs[size:]
+    slope_ref, result_ref, grad_ref, grad_low_ref, sums_ref, acc, flip, seeds = refs[size:]
     step = pl.program_id(0)
     inner = product(low_ref[...], inner_ref[...]) + inner_bias_ref[...].astype(FULL)
     active, slope = gelu_parts(inner)
@@ -313,6 +313,11 @@
     def _():
         acc[...] += part
 
+    deep = first_ref.shape[0]
+    here = pl.ds(pl.multiple_of(step * deep, deep), deep)
+    acc[here, :] += first_ref[...]
+    seeds[here, :] = seed_ref[...]
+
     @pl.when(step == pl.num_programs(0) - 1)
     def _():
         gain = gain_ref[...].astype(FULL)
@@ -321,9 +326,9 @@
 
         def some(block, sums):
             lines = pl.ds(pl.multiple_of(block * LINES, LINES), LINES)
-            unit, factor = norm_stats(first_ref[lines, :] + acc[lines, :] + bias)
+            unit, factor = norm_stats(acc[lines, :] + bias)
             result_ref[lines, :] = (unit * gain + shift).astype(LOW)
-            seed = seed_ref[lines, :].astype(FULL)
+            seed = seeds[lines, :].astype(FULL)
             grad = norm_pull(unit, factor, gain, seed)
             grad_ref[lines, :] = grad
             grad_low_ref[lines, :] = grad.astype(LOW)
@@ -342,6 +347,7 @@
     hidden = inner_weight.shape[1]
     tile = 512
     whole = pl.BlockSpec((rows, width), lambda i, s: (0, 0))
+    line = pl.BlockSpec((rows * tile // hidden, width), lambda i, s: (i, 0))
     across = pl.BlockSpec((rows, tile), lambda i, s: (0, i))
     return pl.pallas_call(
         functools.partial(feed_kernel, size, hidden // number),
@@ -350,8 +356,8 @@
             grid=(hidden // tile,),
             in_specs=[
                 whole,
-                whole,
-                whole,
+                line,
+                line,
                 pl.BlockSpec((width, tile), lambda i, s: (0, i)),
                 pl.BlockSpec((1, tile), lambda i, s: (0, i)),
                 pl.BlockSpec((tile, width), lambda i, s: (i, 0)),
@@ -359,7 +365,8 @@
             + [row_of(k, width) for k in (3, 4, 5)],
             out_specs=[pl.BlockSpec((tile // size, rows), lambda i, s: (i, 0))] * size
             + [across, whole, whole, whole, pl.BlockSpec((8, width), lambda i, s: (0, 0))],
-            scratch_shapes=[pltpu.VMEM((rows, width), FULL), pltpu.VMEM((tile, rows), LOW)],
+            scratch_shapes=[pltpu.VMEM((rows, width), FULL), pltpu.VMEM((tile, rows), LOW)]
+            + [pltpu.VMEM((rows, width), LOW)],
         ),
         out_shape=[jax.ShapeDtypeStruct((hidden // size, rows), LOW)] * size
         + [
@@ -384,7 +391,7 @@
     bias_ref, one_ref, low_ref, sums_ref = refs[size : size + 4]
     cuts = refs[size + 4 : 2 * size + 4]
     mixes = refs[2 * size + 4 : 3 * size + 4]
-    acc, keep = refs[3 * size + 4 :]
+    acc, keep, units, weights = refs[3 * size + 4 :]
     step = pl.program_id(0)
     grad_inner = slope_ref[...].astype(FULL) * right_product(grad_low_ref[...], outer_ref[...])
     bias_ref[...] = column_sum(grad_inner)
@@ -405,14 +412,23 @@
     def _():
         acc[...] += part
 
+    deep = grad_ref.shape[0]
+    here = pl.ds(pl.multiple_of(step * deep, deep), deep)
+    acc[here, :] += grad_ref[...]
+    units[here, :] = unit_ref[...]
+    deep = out_weights[0].shape[0]
+    here = pl.ds(pl.multiple_of(step * deep, deep), deep)
+    for k in range(size):
+        weights[k, here, :] = out_weights[k][...]
+
     @pl.when(step == pl.num_programs(0) - 1)
     def _():
         gain = gain_ref[...].astype(FULL)
 
         def some(block, sums):
             lines = pl.ds(pl.multiple_of(block * LINES, LINES), LINES)
-            grad = grad_ref[lines, :] + acc[lines, :]
-            unit = unit_ref[lines, :]
+            grad = acc[lines, :]
+            unit = units[lines, :]
             one = norm_pull(unit, factor_ref[lines, :], gain, grad)
             one_ref[lines, :] = one
             low = one.astype(LOW)
@@ -428,7 +444,7 @@
         for k in range(size):
             spot = pl.multiple_of((place_ref[1] ^ k) * share, 128)
             cuts[k][...] = keep[:, pl.ds(spot, share)]
-            mixes[k][...] = right_product(low, out_weights[k][...]).astype(LOW)
+            mixes[k][...] = right_product(low, weights[k]).astype(LOW)
 
 
 def feed_back(
@@ -449,6 +465,7 @@
         return pl.BlockSpec((rows, tile), lambda i, s: (0, jnp.clip(i - start, 0, steps - 1)))
 
     whole = pl.BlockSpec((rows, width), lambda i, s: (0, 0))
+    line = pl.BlockSpec((rows * tile // hidden, width), lambda i, s: (i, 0))
     return pl.pallas_call(
         functools.partial(feed_back_kernel, size, steps, share),
         grid_spec=pltpu.PrefetchScalarGridSpec(
@@ -456,15 +473,15 @@
             grid=(hidden // tile,),
             in_specs=[
                 whole,
-                whole,
+                line,
                 pl.BlockSpec((rows, tile), lambda i, s: (0, spot(i, s))),
                 pl.BlockSpec((width, tile), lambda i, s: (0, spot(i, s))),
                 pl.BlockSpec((tile, width), lambda i, s: (spot(i, s), 0)),
-                whole,
+                line,
                 pl.BlockSpec((rows, 1), lambda i, s: (0, 0)),
                 row_of(1, width),
             ]
-            + [pl.BlockSpec((share, width), lambda i, s: (0, 0))] * size,
+            + [pl.BlockSpec((share * tile // hidden, width), lambda i, s: (i, 0))] * size,
             out_specs=[own(k) for k in range(size)]
             + [
                 pl.BlockSpec((1, tile), lambda i, s: (0, spot(i, s))),
@@ -473,7 +490,12 @@
                 pl.BlockSpec((8, width), lambda i, s: (0, 0)),
             ]
             + [pl.BlockSpec((rows, share), lambda i, s: (0, 0))] * (2 * size),
-            scratch_shapes=[pltpu.VMEM((rows, width), FULL), pltpu.VMEM((rows, width), LOW)],
+            scratch_shapes=[
+                pltpu.VMEM((rows, width), FULL),
+                pltpu.VMEM((rows, width), LOW),
+                pltpu.VMEM((rows, width), FULL),
+                pltpu.VMEM((size, share, width), LOW),
+            ],
         ),
         out_shape=[jax.ShapeDtypeStruct((rows, part), LOW)] * size
         + [
@@ -721,8 +743,7 @@
 
 
 def fold_kernel(counts, *refs):
-    total = 4 * sum(counts)
-    outs = refs[total:]
+    outs = refs[4 * sum(counts) :]
     spot = 0
     for k, count in enumerate(counts):
         start = 0
@@ -737,13 +758,14 @@
             start, spot = start + deep, spot + 4
 
 
-def fold(*groups):
-    orders = []
+def fold(*groups, join=False):
+    skip = 1 if join else 0
+    merged = {}
     for group in groups:
         for part in group:
-            if part["order"] not in orders:
-                orders.append(part["order"])
-    merged = [[p for g in groups for p in g if p["order"] == order] for order in orders]
+            key = str([o[skip:] for o in part["order"]])
+            merged.setdefault(key, []).append(part)
+    merged = list(merged.values())
     half = merged[0][0]["near"].shape[0] // 2
     operands, in_specs, out_specs, out_shape, counts = [], [], [], [], []
     for parts in merged:
@@ -764,7 +786,7 @@
         in_specs=in_specs,
         out_specs=out_specs,
         out_shape=out_shape,
-        compiler_params=params(60 if len(operands) > 16 else 40),
+        compiler_params=params(48 if len(operands) > 16 else 40),
         cost_estimate=CHEAP,
         name="fold",
     )(*operands)
@@ -1095,7 +1117,7 @@
     input_grad = wide(home_grad)
     late = after(late, input_grad, outer_weight_grad)
     while len(late[0]["order"][0]) > 1:
-        late = fold(late)
+        late = fold(late, join=len(late[0]["order"][0]) == 2)
         early_away = tie(early_away, far(late))
         late = send(late)
     early = [early[0]] + early_away

time: 290 us -> 284 us (0.979)
  local copies, waits for them, and re-layouts: 31.2 us -> 23.9 us
  waiting for transfers between devices: 41.7 us -> 49 us
  Pallas kernels: 154 us -> 148 us
    unnamed x144 -> x116, local copies, waits for them, and re-layouts: 23.9 us -> 16.4 us
    ppermute x21 -> x20, waiting for transfers between devices: 35.4 us -> 41.6 us  [send(): lax.ppermute(p['far'], BOTH, [(i, i ^ size << p['order'][i % size % 2][0]...]
    ppermute x21 -> x20, starting transfers between devices: 29.7 us -> 27.9 us  [send(): lax.ppermute(p['far'], BOTH, [(i, i ^ size << p['order'][i % size % 2][0]...]
  transfers between devices with their start and end apart: 36 -> 35, of which waited for: 19 -> 17; matrix products, arithmetic and copies ran while one was open for 6% -> 7% of each run, Pallas kernels for 34% -> 34%
where the time goes in v1:
time: 284 us; the launch traced here: 282 us
  Pallas kernels  148 us (52%)
  waiting for transfers between devices  49 us (17%)
  starting transfers between devices  44.1 us (16%)
  local copies, waits for them, and re-layouts  23.9 us (8%)
  other arithmetic  12.9 us (5%)
  matrix products  3.41 us (1%)
    ppermute x20, waiting for transfers between devices, send(): lax.ppermute(p['far'], BOTH, [(i, i ^ size << p['order'][i % size % 2][0]...  41.6 us
    pallas_call x5, Pallas kernels, weight_grad(): pl.pallas_call(functools.partial(weight_kernel, [len(m) for m in lefts],...  34.3 us
    ppermute x20, starting transfers between devices, send(): lax.ppermute(p['far'], BOTH, [(i, i ^ size << p['order'][i % size % 2][0]...  27.9 us
    pallas_call x1, Pallas kernels, feed_forward(): pl.pallas_call(functools.partial(feed_kernel, size, hidden // number), gr...  25.5 us
    pallas_call x2, Pallas kernels, attention_backward(): pl.pallas_call(functools.partial(backward_kernel, members), grid=(count,...  24.9 us
    pallas_call x1, Pallas kernels, feed_back(): pl.pallas_call(functools.partial(feed_back_kernel, size, steps, share), g...  24.5 us
    unnamed x116, local copies, waits for them, and re-layouts  16.4 us
    pallas_call x1, Pallas kernels, attention_forward(): pl.pallas_call(forward_kernel, grid=(pairs, rows // tile), in_specs=[line...  13.9 us
  transfers between devices with their start and end apart: 35, of which 17 were waited for; matrix products, arithmetic and copies ran while one was open for 7% of the time, Pallas kernels for 34%

profile of v1, /device:TPU:0, one launch (start us, length us, event | category | flops | bytes accessed | tf_op | source)
XLA Modules:
  0.0 282.5 jit_solution(14626887528886655868)
XLA Ops:
  0.7 5.2 %all-to-all-start = ((bf16[8,64,1024]{2,1,0:T(8,128)(2,1)}), bf16[8,64,1024]{2,1,0:T(8,128)(2,1)}, u32[]{:S(2)}, u32[]{:S(2)}) async-start(bf16[8,64,1024]{2,1,0:T(8,128)(2,1)} %bitcast.79), calls=%async_computation | async-start | bytes 2097152 | tf_op jit(solution)/shard_map/all_to_all | solution.py:952
  5.9 2.6 copy.40.replace_ref
  8.6 2.2 copy.41.cotangent_ref
  10.9 1.7 copy-done.11
  12.6 1.9 masked_rows.1
  14.5 1.0 copy-done.28
  15.5 1.0 copy-done.29
  18.0 3.3 %constant_dynamic-slice_fusion.3 = (bf16[512,1024]{1,0:T(8,128)(2,1)}, bf16[512,1024]{1,0:T(8,128)(2,1)}) fusion(bf16[1024,1024]{1,0:T(8,128)(2,1)} %param.30, s32[]{:T(128)S(6)} %select_n.115, s32[]{:T(128)S(6)} %select_n.114), kind=kLoop, calls=%fused_computation.55 | loop fusion | bytes 4194312 | tf_op jit(solution)/shard_map/dynamic_slice | solution.py:909
  21.4 1.5 bitcast_select_fusion.current_ref.refs_0_
  24.1 1.6 collective-permute-done.refs_1_
  25.7 3.4 %add_convert_fusion.query_ref.key_ref.value_ref = bf16[1024,1536]{1,0:T(8,128)(2,1)S(1)} fusion(f32[1536]{0:T(1024)S(1)} %maximum_convert_fusion, bf16[512,1024]{1,0:T(8,128)(2,1)S(1)} %collective-permute-done.refs_1_, bf16[512,1024]{1,0:T(8,128)(2,1)S(1)} %bitcast_select_fusion.current_ref.refs_0_, bf16[1024,512]{1,0:T(8,128)(2,1)S(1)} %get-tuple-element.301, ...), kind=kOutput, calls=%fused_computation | convolution fusion | flops 3238002688 | bytes 8394752 | tf_op jit(solution)/shard_map/dot_general | solution.py:23
  29.2 1.0 copy-done.13
  30.2 13.9 %attention_forward.1 = (bf16[1024,512]{1,0:T(8,128)(2,1)S(1)}, f32[4,2,1024]{2,1,0:T(2,128)S(1)}) custom-call(bf16[1024,1536]{1,0:T(8,128)(2,1)S(1)} %add_convert_fusion.query_ref.key_ref.value_ref, bf16[1024,1536]{1,0:T(8,128)(2,1)S(1)} %add_convert_fusion.query_ref.key_ref.value_ref, bf16[1024,1536]{1,0:T(8,128)(2,1)S(1)} %add_convert_fusion.query_ref.key_ref.value_ref), custom_call_target="tpu_custom_call" | custom-call | flops 1 | bytes 1 | tf_op jit(solution)/shard_map/attention_forward/pallas_call | solution.py:141
  44.0 1.0 copy-done
  45.0 1.0 fusion.22
  47.0 1.3 collective-permute-done.1.refs_1_
  48.3 5.9 %first_half.1 = (f32[512,1024]{1,0:T(8,128)}, bf16[1024,512]{1,0:T(8,128)(2,1)}, bf16[512,1024]{1,0:T(8,128)(2,1)}, f32[512,1024]{1,0:T(8,128)}, f32[512,1]{1,0:T(8,128)}) custom-call(bf16[512,1024]{1,0:T(8,128)(2,1)} %copy-done.3, f32[6,1,1024]{2,1,0:T(1,128)} %convert_element_type.32.bias_ref.gain_ref.shift_ref.outer_bias_ref, ...), custom_call_target="tpu_custom_call" | custom-call | flops 1 | bytes 1 | tf_op jit(solution)/shard_map/first_half/pallas_call | solution.py:262
  54.2 25.5 %feed_forward.1 = (bf16[2048,512]{1,0:T(8,128)(2,1)}, bf16[2048,512]{1,0:T(8,128)(2,1)}, bf16[512,4096]{1,0:T(8,128)(2,1)}, bf16[512,1024]{1,0:T(8,128)(2,1)}, f...) custom-call(s32[2]{0:T(128)} %pad_add_fusion.place_ref, ...), custom_call_target="tpu_custom_call" | custom-call | flops 1 | bytes 1 | tf_op jit(solution)/shard_map/feed_forward/pallas_call | solution.py:352
  80.3 4.2 %all-to-all-start.1 = ((bf16[8,64,1024]{2,1,0:T(8,128)(2,1)}), bf16[8,64,1024]{2,1,0:T(8,128)(2,1)}, u32[]{:S(2)}, u32[]{:S(2)}) async-start(bf16[8,64,1024]{2,1,0:T(8,128)(2,1)} %bitcast.80), calls=%async_computation.1 | async-start | bytes 2097152 | tf_op jit(solution)/shard_map/all_to_all | solution.py:1007
  84.5 24.5 %feed_back.1 = (bf16[512,2048]{1,0:T(8,128)(2,1)}, bf16[512,2048]{1,0:T(8,128)(2,1)}, f32[1,4096]{1,0:T(1,128)}, f32[512,1024]{1,0:T(8,128)}, bf16[512,1024]{1,0...) custom-call(s32[2]{0:T(128)} %pad_add_fusion.place_ref, ...), custom_call_target="tpu_custom_call" | custom-call | flops 1 | bytes 1 | tf_op jit(solution)/shard_map/feed_back/pallas_call | solution.py:469
  109.5 9.5 %weight_grad.5 = (bf16[8,4,80,256]{3,2,1,0:T(8,128)(2,1)}, bf16[8,4,80,256]{3,2,1,0:T(8,128)(2,1)}, bf16[8,4,48,256]{3,2,1,0:T(8,128)(2,1)}, bf16[8,4,48,256]{3,2,1,0:T(8,128)(2,1)}) custom-call(s32[2]{0:T(128)} %pad_add_fusion.place_ref, bf16[2048,512]{1,0:T(8,128)(2,1)} %get-tuple-element.173.refs_0_, bf16[2048,512]{1,0:T(8,128)(2,1)} %collective-permute-done.3.refs_1_, ...), custom_call_target="tpu_custom_call" | custom-call | flops 1 | bytes 1 | tf_op jit(solution)/shard_map/weight_grad/pallas_call | solution.py:693
  119.1 1.7 collective-permute-start.8
  121.3 2.0 collective-permute-start.9
  123.8 1.7 collective-permute-done.6.refs_5_
  125.5 5.3 %weight_grad.6 = (bf16[8,2,64,256]{3,2,1,0:T(8,128)(2,1)}, bf16[8,2,64,256]{3,2,1,0:T(8,128)(2,1)}) custom-call(s32[2]{0:T(128)} %pad_add_fusion.1.place_ref, bf16[1024,512]{1,0:T(8,128)(2,1)} %copy-done, bf16[512,512]{1,0:T(8,128)(2,1)} %collective-permute-done.1.refs_1_, bf16[1024,512]{1,0:T(8,128)(2,1)} %copy-done, ...), custom_call_target="tpu_custom_call" | custom-call | flops 1 | bytes 1 | tf_op jit(solution)/shard_map/weight_grad/pallas_call | solution.py:693
  130.8 11.3 %weight_grad.7 = (bf16[8,8,48,256]{3,2,1,0:T(8,128)(2,1)}, bf16[8,8,48,256]{3,2,1,0:T(8,128)(2,1)}, bf16[8,9,16,256]{3,2,1,0:T(8,128)(2,1)}, bf16[8,9,16,256]{3,2,1,0:T(8,128)(2,1)}) custom-call(s32[2]{0:T(128)} %pad_add_fusion.place_ref, bf16[1024,512]{1,0:T(8,128)(2,1)} %get-tuple-element.170.refs_0_, bf16[1024,512]{1,0:T(8,128)(2,1)} %collective-permute-done.4.refs_1_, ...), custom_call_target="tpu_custom_call" | custom-call | flops 1 | bytes 1 | tf_op jit(solution)/shard_map/weight_grad/pallas_call | solution.py:693
  142.2 1.5 collective-permute-start.11
  143.7 2.0 collective-permute-start.12
  146.0 1.8 collective-permute-done.10.refs_1_
  147.8 1.4 copy-done.1
  149.2 12.5 %attention_backward.2.refs_2_.refs_3_ = bf16[3,1024,512]{2,1,0:T(8,128)(2,1)S(1)} custom-call(bf16[1024,1536]{1,0:T(8,128)(2,1)S(1)} %add_convert_fusion.query_ref.key_ref.value_ref, bf16[1024,1536]{1,0:T(8,128)(2,1)S(1)} %add_convert_fusion.query_ref.key_ref.value_ref, bf16[1024,1536]{1,0:T(8,128)(2,1)S(1)} %add_convert_fusion.query_ref.key_ref.value_ref, ...), custom_call_target="tpu_custom_call" | custom-call | flops 1 | bytes 1 | tf_op jit(solution)/shard_map/attention_backward/pallas_call | solution.py:170
  161.8 4.1 %weight_grad.8 = (bf16[8,3,48,256]{3,2,1,0:T(8,128)(2,1)S(1)}, bf16[8,3,48,256]{3,2,1,0:T(8,128)(2,1)S(1)}, bf16[8,4,16,256]{3,2,1,0:T(8,128)(2,1)S(1)}, bf16[8,4,16,256]{3,2,1,0:T(8,128)(2,1)S(1)}) custom-call(s32[2]{0:T(128)S(1)} %copy-done.39, bf16[512,1024]{1,0:T(8,128)(2,1)S(1)} %copy-done.4, bf16[512,1024]{1,0:T(8,128)(2,1)S(1)} %copy-done.14, ...), custom_call_target="tpu_custom_call" | custom-call | flops 1 | bytes 1 | tf_op jit(solution)/shard_map/weight_grad/pallas_call | solution.py:693
  165.9 0.9 copy-done.18
  167.5 1.0 collective-permute-done.13.refs_10_.refs_11_
  168.5 1.1 copy-done.41
  169.7 5.5 %fold.6 = (bf16[4,832,256]{2,1,0:T(8,128)(2,1)}, bf16[4,832,256]{2,1,0:T(8,128)(2,1)}, bf16[4,336,256]{2,1,0:T(8,128)(2,1)S(1)}, bf16[4,336,256]{2,1,0:T(8,128)(2,1)}) custom-call(bf16[8,320,256]{2,1,0:T(8,128)(2,1)} %bitcast.77, bf16[8,320,256]{2,1,0:T(8,128)(2,1)} %bitcast.78, bf16[8,320,256]{2,1,0:T(8,128)(2,1)} %collective-permute-done.8.refs_2_.refs_3_, ...), custom_call_target="tpu_custom_call" | custom-call | flops 1 | bytes 1 | tf_op jit(solution)/shard_map/fold/pallas_call | solution.py:783
  175.2 1.8 collective-permute-start.14
  177.0 2.0 collective-permute-start.15
  179.3 1.0 copy-done.27
  180.3 12.5 %attention_backward.3.refs_2_.refs_3_.refs_0_ = bf16[3,1024,512]{2,1,0:T(8,128)(2,1)S(1)} custom-call(bf16[1024,1536]{1,0:T(8,128)(2,1)S(1)} %add_convert_fusion.query_ref.key_ref.value_ref, bf16[1024,1536]{1,0:T(8,128)(2,1)S(1)} %add_convert_fusion.query_ref.key_ref.value_ref, ...), custom_call_target="tpu_custom_call", output_to_operand_aliasing={{}: (7, {})} | custom-call | flops 1 | bytes 1 | tf_op jit(solution)/shard_map/attention_backward/pallas_call | solution.py:170
  192.8 10.1 %collective-permute-done.17.refs_10_.refs_11_ = bf16[8,64,256]{2,1,0:T(8,128)(2,1)S(1)} collective-permute-done((bf16[8,64,256]{2,1,0:T(8,128)(2,1)S(1)}, bf16[8,64,256]{2,1,0:T(8,128)(2,1)S(1)}, u32[]{:S(2)}, u32[]{:S(2)}) %collective-permute-start.17) | collective-permute-done | bytes 262176 | tf_op jit(solution)/shard_map/ppermute | solution.py:931
  204.0 1.7 collective-permute-start.19
  206.1 4.1 %weight_grad.9 = (bf16[8,3,48,256]{3,2,1,0:T(8,128)(2,1)S(1)}, bf16[8,3,48,256]{3,2,1,0:T(8,128)(2,1)S(1)}, bf16[8,4,16,256]{3,2,1,0:T(8,128)(2,1)S(1)}, bf16[8,4,16,256]{3,2,1,0:T(8,128)(2,1)S(1)}) custom-call(s32[2]{0:T(128)S(1)} %copy-done.39, bf16[512,1024]{1,0:T(8,128)(2,1)S(1)} %copy-done.4, bf16[512,1024]{1,0:T(8,128)(2,1)S(1)} %copy-done.15, ...), custom_call_target="tpu_custom_call" | custom-call | flops 1 | bytes 1 | tf_op jit(solution)/shard_map/weight_grad/pallas_call | solution.py:693
  210.2 5.7 %collective-permute-done.20.refs_6_.refs_7_ = bf16[2,336,256]{2,1,0:T(8,128)(2,1)S(1)} collective-permute-done((bf16[2,336,256]{2,1,0:T(8,128)(2,1)S(1)}, bf16[2,336,256]{2,1,0:T(8,128)(2,1)S(1)}, u32[]{:S(2)}, u32[]{:S(2)}) %collective-permute-start.20) | collective-permute-done | bytes 344096 | tf_op jit(solution)/shard_map/ppermute | solution.py:931
  215.9 0.8 collective-permute-done.19.refs_2_.refs_3_
  216.8 1.4 collective-permute-start.21
  218.5 3.0 %collective-permute-start.23 = (bf16[1,832,256]{2,1,0:T(8,128)(2,1)S(1)}, bf16[1,832,256]{2,1,0:T(8,128)(2,1)}, u32[]{:S(2)}, u32[]{:S(2)}) collective-permute-start(bf16[1,832,256]{2,1,0:T(8,128)(2,1)S(1)} %get-tuple-element.225), channel_id=1, source_target_pairs={{0,16},{1,17},{2,18},{3,19},{4,20},{5,21},{6,22},{7,23},{8,24},{9,... | collective-permute-start | bytes 1277960 | tf_op jit(solution)/shard_map/ppermute | solution.py:931
  221.5 1.6 collective-permute-start.22
  223.1 5.7 %input_back.1 = bf16[512,1024]{1,0:T(8,128)(2,1)} custom-call(s32[2]{0:T(128)S(1)} %copy-done.39, f32[512,1024]{1,0:T(8,128)S(1)} %copy-done.22, f32[512,1]{1,0:T(8,128)S(1)} %get-tuple-element.142.masked_ref, bf16[3,1024,512]{2,1,0:T(8,128)(2,1)S(1)} %attention_backward.3.refs_2_.refs_3_.refs_0_, bf16[3,512,512]{2,1,0:T(8,128)(2,1)S(1)} %collective-permute-done.18.refs_1_, ...), custom_call_target="tpu_custom_call" | custom-call | flops 1 | bytes 1 | tf_op jit(solution)/shard_map/input_back/pallas_call | solution.py:529
  228.8 4.2 %all-to-all-start.2 = ((bf16[8,64,1024]{2,1,0:T(8,128)(2,1)}), bf16[8,64,1024]{2,1,0:T(8,128)(2,1)}, u32[]{:S(2)}, u32[]{:S(2)}) async-start(bf16[8,64,1024]{2,1,0:T(8,128)(2,1)} %bitcast.22), calls=%async_computation.2 | async-start | bytes 2097152 | tf_op jit(solution)/shard_map/all_to_all | solution.py:1007
  233.1 2.9 %bitcast_convert_fusion.1 = f32[4,128,1024]{2,1,0:T(8,128)} fusion(bf16[4,128,1024]{2,1,0:T(8,128)(2,1)} %bitcast.56), kind=kLoop, calls=%fused_computation.6 | loop fusion | flops 524288 | bytes 3145728 | tf_op jit(solution)/shard_map/convert_element_type | solution.py:1010
  236.0 4.0 %collective-permute-done.23.refs_1_ = bf16[1,832,256]{2,1,0:T(8,128)(2,1)} collective-permute-done((bf16[1,832,256]{2,1,0:T(8,128)(2,1)S(1)}, bf16[1,832,256]{2,1,0:T(8,128)(2,1)}, u32[]{:S(2)}, u32[]{:S(2)}) %collective-permute-start.23) | collective-permute-done | bytes 426016 | tf_op jit(solution)/shard_map/ppermute | solution.py:931
  240.1 1.9 fold.9
  243.1 3.5 %collective-permute-start.26 = (bf16[1,336,256]{2,1,0:T(8,128)(2,1)S(1)}, bf16[1,336,256]{2,1,0:T(8,128)(2,1)S(1)}, u32[]{:S(2)}, u32[]{:S(2)}) collective-permute-start(bf16[1,336,256]{2,1,0:T(8,128)(2,1)S(1)} %get-tuple-element.242), channel_id=1, source_target_pairs={{0,16},{1,17},{2,18},{3,19},{4,20},{5,21},{6,22},{7,23},{8,24},{9,... | collective-permute-start | bytes 516104 | tf_op jit(solution)/shard_map/ppermute | solution.py:931
  246.6 6.2 %collective-permute-done.26.refs_3_ = bf16[1,336,256]{2,1,0:T(8,128)(2,1)S(1)} collective-permute-done((bf16[1,336,256]{2,1,0:T(8,128)(2,1)S(1)}, bf16[1,336,256]{2,1,0:T(8,128)(2,1)S(1)}, u32[]{:S(2)}, u32[]{:S(2)}) %collective-permute-start.26) | collective-permute-done | bytes 172064 | tf_op jit(solution)/shard_map/ppermute | solution.py:931
  253.1 2.7 collective-permute-done.24.refs_2_.refs_3_
  256.0 1.9 final.2
  258.3 1.6 collective-permute-start.28
  259.9 2.8 bitcast_convert_fusion
  262.7 1.0 collective-permute-done.28.refs_6_.refs_7_
  263.7 0.9 collective-permute-done.27.refs_2_.refs_3_
  264.7 1.7 collective-permute-start.29
  268.7 8.8 %collective-permute-done.29.refs_1_ = bf16[1,416,256]{2,1,0:T(8,128)(2,1)S(1)} collective-permute-done((bf16[1,416,256]{2,1,0:T(8,128)(2,1)S(1)}, bf16[1,416,256]{2,1,0:T(8,128)(2,1)S(1)}, u32[]{:S(2)}, u32[]{:S(2)}) %collective-permute-start.29) | collective-permute-done | bytes 213024 | tf_op jit(solution)/shard_map/ppermute | solution.py:931
  278.8 1.0 collective-permute-done.31
  (187 shorter events, 17.4 us)
Async XLA Ops:
  0.7 20.7 %all-to-all-start = ((bf16[8,64,1024]{2,1,0:T(8,128)(2,1)}), bf16[8,64,1024]{2,1,0:T(8,128)(2,1)}, u32[]{:S(2)}, u32[]{:S(2)}) async-start(bf16[8,64,1024]{2,1,0:T(8,128)(2,1)} %bitcast.79), calls=%async_computation | async-start | bytes 2097152 | tf_op jit(solution)/shard_map/all_to_all | solution.py:952
  12.6 3.9 %copy-start.49 = (bf16[1024]{0:T(1024)(128)(2,1)S(1)}, bf16[1024]{0:T(1024)(128)(2,1)}, u32[]{:S(2)}) copy-start(bf16[1024]{0:T(1024)(128)(2,1)} %param.37) | copy-start | bytes 6148
  12.6 3.9 %copy-start.50 = (bf16[1024]{0:T(1024)(128)(2,1)S(1)}, bf16[1024]{0:T(1024)(128)(2,1)}, u32[]{:S(2)}) copy-start(bf16[1024]{0:T(1024)(128)(2,1)} %param.38) | copy-start | bytes 6148
  12.6 3.9 %copy-start.51 = (bf16[1024]{0:T(1024)(128)(2,1)S(1)}, bf16[1024]{0:T(1024)(128)(2,1)}, u32[]{:S(2)}) copy-start(bf16[1024]{0:T(1024)(128)(2,1)} %param.39) | copy-start | bytes 6148
  12.6 4.6 %copy-start.44 = (bf16[4096]{0:T(1024)(128)(2,1)S(1)}, bf16[4096]{0:T(1024)(128)(2,1)}, u32[]{:S(2)}) copy-start(bf16[4096]{0:T(1024)(128)(2,1)} %param.35) | copy-start | bytes 24580
  18.0 5.6 %copy-start.9 = (bf16[1024,1024]{1,0:T(8,128)(2,1)S(1)}, bf16[1024,1024]{1,0:T(8,128)(2,1)}, u32[]{:S(2)}) copy-start(bf16[1024,1024]{1,0:T(8,128)(2,1)} %refs_5_.1) | copy-start | bytes 6291460
  22.9 2.8 collective-permute-start
  46.0 2.3 collective-permute-start.1
  79.7 29.4 %collective-permute-start.3 = (bf16[2048,512]{1,0:T(8,128)(2,1)}, bf16[2048,512]{1,0:T(8,128)(2,1)}, u32[]{:S(2)}, u32[]{:S(2)}) collective-permute-start(bf16[2048,512]{1,0:T(8,128)(2,1)} %get-tuple-element.165), channel_id=1, source_target_pairs={{0,1},{1,0},{2,3},{3,2},{4,5},{5,4},{6,7},{7,6},{8,9},{9,8},{10,11... | collective-permute-start | bytes 6291464 | tf_op jit(solution)/shard_map/ppermute | solution.py:906
  80.1 28.9 %collective-permute-start.2 = (bf16[512,1024]{1,0:T(8,128)(2,1)}, bf16[512,1024]{1,0:T(8,128)(2,1)}, u32[]{:S(2)}, u32[]{:S(2)}) collective-permute-start(bf16[512,1024]{1,0:T(8,128)(2,1)} %get-tuple-element.175.grad_low_ref.refs_2_), channel_id=1, source_target_pairs={{0,1},{1,0},{2,3},{3,2},{4,5},{5,4},{6,7},{7,6},{8,9},{9,8},{10,11... | collective-permute-start | bytes 3145736 | tf_op jit(solution)/shard_map/ppermute | solution.py:906
  80.3 28.8 %all-to-all-start.1 = ((bf16[8,64,1024]{2,1,0:T(8,128)(2,1)}), bf16[8,64,1024]{2,1,0:T(8,128)(2,1)}, u32[]{:S(2)}, u32[]{:S(2)}) async-start(bf16[8,64,1024]{2,1,0:T(8,128)(2,1)} %bitcast.80), calls=%async_computation.1 | async-start | bytes 2097152 | tf_op jit(solution)/shard_map/all_to_all | solution.py:1007
  109.1 11.7 %copy-start.43 = (bf16[512,512]{1,0:T(8,128)(2,1)S(1)}, bf16[512,512]{1,0:T(8,128)(2,1)}, u32[]{:S(2)}) copy-start(bf16[512,512]{1,0:T(8,128)(2,1)} %get-tuple-element.269) | copy-start | bytes 1572868
  109.1 21.7 %collective-permute-start.7 = (bf16[512,2048]{1,0:T(8,128)(2,1)}, bf16[512,2048]{1,0:T(8,128)(2,1)}, u32[]{:S(2)}, u32[]{:S(2)}) collective-permute-start(bf16[512,2048]{1,0:T(8,128)(2,1)} %get-tuple-element.183), channel_id=1, source_target_pairs={{0,1},{1,0},{2,3},{3,2},{4,5},{5,4},{6,7},{7,6},{8,9},{9,8},{10,11... | collective-permute-start | bytes 6291464 | tf_op jit(solution)/shard_map/ppermute | solution.py:906
  119.1 23.1 %collective-permute-start.8 = (bf16[8,320,256]{2,1,0:T(8,128)(2,1)}, bf16[8,320,256]{2,1,0:T(8,128)(2,1)}, u32[]{:S(2)}, u32[]{:S(2)}) collective-permute-start(bf16[8,320,256]{2,1,0:T(8,128)(2,1)} %bitcast.84), channel_id=1, source_target_pairs={{0,2},{1,5},{2,0},{3,7},{4,6},{5,1},{6,4},{7,3},{8,10},{9,13},{10,... | collective-permute-start | bytes 3932168 | tf_op jit(solution)/shard_map/ppermute | solution.py:931
  120.7 2.5 collective-permute-start.5
  120.8 10.0 %collective-permute-start.4 = (bf16[1024,512]{1,0:T(8,128)(2,1)}, bf16[1024,512]{1,0:T(8,128)(2,1)}, u32[]{:S(2)}, u32[]{:S(2)}) collective-permute-start(bf16[1024,512]{1,0:T(8,128)(2,1)} %get-tuple-element.170.refs_0_), channel_id=1, source_target_pairs={{0,1},{1,0},{2,3},{3,2},{4,5},{5,4},{6,7},{7,6},{8,9},{9,8},{10,11... | collective-permute-start | bytes 3145736 | tf_op jit(solution)/shard_map/ppermute | solution.py:906
  121.3 20.9 %collective-permute-start.9 = (bf16[8,192,256]{2,1,0:T(8,128)(2,1)}, bf16[8,192,256]{2,1,0:T(8,128)(2,1)}, u32[]{:S(2)}, u32[]{:S(2)}) collective-permute-start(bf16[8,192,256]{2,1,0:T(8,128)(2,1)} %bitcast.85), channel_id=1, source_target_pairs={{0,8},{1,9},{2,10},{3,11},{4,12},{5,13},{6,14},{7,15},{8,0},{9,1},... | collective-permute-start | bytes 2359304 | tf_op jit(solution)/shard_map/ppermute | solution.py:931
  123.2 2.3 collective-permute-start.6
  130.8 17.0 %copy-start.23 = (bf16[512,512]{1,0:T(8,128)(2,1)S(1)}, bf16[512,512]{1,0:T(8,128)(2,1)}, u32[]{:S(2)}) copy-start(bf16[512,512]{1,0:T(8,128)(2,1)} %get-tuple-element.191.refs_0_) | copy-start | bytes 1572868
  142.2 26.3 %collective-permute-start.11 = (bf16[8,384,256]{2,1,0:T(8,128)(2,1)}, bf16[8,384,256]{2,1,0:T(8,128)(2,1)S(1)}, u32[]{:S(2)}, u32[]{:S(2)}) collective-permute-start(bf16[8,384,256]{2,1,0:T(8,128)(2,1)} %bitcast.83), channel_id=1, source_target_pairs={{0,2},{1,5},{2,0},{3,7},{4,6},{5,1},{6,4},{7,3},{8,10},{9,13},{10,... | collective-permute-start | bytes 4718600 | tf_op jit(solution)/shard_map/ppermute | solution.py:931
  143.7 24.8 %collective-permute-start.12 = (bf16[8,144,256]{2,1,0:T(8,128)(2,1)}, bf16[8,144,256]{2,1,0:T(8,128)(2,1)S(1)}, u32[]{:S(2)}, u32[]{:S(2)}) collective-permute-start(bf16[8,144,256]{2,1,0:T(8,128)(2,1)} %bitcast.86), channel_id=1, source_target_pairs={{0,8},{1,9},{2,10},{3,11},{4,12},{5,13},{6,14},{7,15},{8,0},{9,1},... | collective-permute-start | bytes 1769480 | tf_op jit(solution)/shard_map/ppermute | solution.py:931
  145.7 2.1 collective-permute-start.10
  145.7 22.8 %collective-permute-start.13 = (bf16[8,128,256]{2,1,0:T(8,128)(2,1)}, bf16[8,128,256]{2,1,0:T(8,128)(2,1)S(1)}, u32[]{:S(2)}, u32[]{:S(2)}) collective-permute-start(bf16[8,128,256]{2,1,0:T(8,128)(2,1)} %bitcast.87), channel_id=1, source_target_pairs={{0,2},{1,5},{2,0},{3,7},{4,6},{5,1},{6,4},{7,3},{8,10},{9,13},{10,... | collective-permute-start | bytes 1572872 | tf_op jit(solution)/shard_map/ppermute | solution.py:931
  147.8 13.9 %copy-start.26 = (bf16[512,512]{1,0:T(8,128)(2,1)}, bf16[512,512]{1,0:T(8,128)(2,1)S(1)}, u32[]{:S(2)}) copy-start(bf16[512,512]{1,0:T(8,128)(2,1)S(1)} %collective-permute-done.10.refs_1_) | copy-start | bytes 1572868
  149.2 12.5 %copy-start.4 = (bf16[512,1024]{1,0:T(8,128)(2,1)S(1)}, bf16[512,1024]{1,0:T(8,128)(2,1)}, u32[]{:S(2)}) copy-start(bf16[512,1024]{1,0:T(8,128)(2,1)} %copy-done.3) | copy-start | bytes 3145732
  149.2 12.5 %copy-start.14 = (bf16[512,1024]{1,0:T(8,128)(2,1)S(1)}, bf16[512,1024]{1,0:T(8,128)(2,1)}, u32[]{:S(2)}) copy-start(bf16[512,1024]{1,0:T(8,128)(2,1)} %copy-done.13) | copy-start | bytes 3145732
  149.2 12.5 %copy-start.39 = (s32[2]{0:T(128)S(1)}, s32[2]{0:T(128)}, u32[]{:S(2)}) copy-start(s32[2]{0:T(128)} %pad_add_fusion.place_ref) | copy-start | bytes 28
  161.7 7.9 %copy-start.16 = (bf16[8,4,48,256]{3,2,1,0:T(8,128)(2,1)S(1)}, bf16[8,4,48,256]{3,2,1,0:T(8,128)(2,1)}, u32[]{:S(2)}) copy-start(bf16[8,4,48,256]{3,2,1,0:T(8,128)(2,1)} %get-tuple-element.203) | copy-start | bytes 2359300
  161.7 7.9 %copy-start.17 = (bf16[8,9,16,256]{3,2,1,0:T(8,128)(2,1)S(1)}, bf16[8,9,16,256]{3,2,1,0:T(8,128)(2,1)}, u32[]{:S(2)}) copy-start(bf16[8,9,16,256]{3,2,1,0:T(8,128)(2,1)} %get-tuple-element.205) | copy-start | bytes 1769476
  161.7 7.9 %copy-start.25 = (bf16[8,2,64,256]{3,2,1,0:T(8,128)(2,1)S(1)}, bf16[8,2,64,256]{3,2,1,0:T(8,128)(2,1)}, u32[]{:S(2)}) copy-start(bf16[8,2,64,256]{3,2,1,0:T(8,128)(2,1)} %get-tuple-element.201) | copy-start | bytes 1572868
  169.6 9.7 %copy-start.2 = (bf16[1024,512]{1,0:T(8,128)(2,1)S(1)}, bf16[1024,512]{1,0:T(8,128)(2,1)}, u32[]{:S(2)}) copy-start(bf16[1024,512]{1,0:T(8,128)(2,1)} %copy-done) | copy-start | bytes 3145732
  169.6 9.7 %copy-start.24 = (bf16[512,512]{1,0:T(8,128)(2,1)S(1)}, bf16[512,512]{1,0:T(8,128)(2,1)}, u32[]{:S(2)}) copy-start(bf16[512,512]{1,0:T(8,128)(2,1)} %get-tuple-element.191.refs_0_) | copy-start | bytes 1572868
  175.2 27.7 %collective-permute-start.14 = (bf16[4,832,256]{2,1,0:T(8,128)(2,1)}, bf16[4,832,256]{2,1,0:T(8,128)(2,1)S(1)}, u32[]{:S(2)}, u32[]{:S(2)}) collective-permute-start(bf16[4,832,256]{2,1,0:T(8,128)(2,1)} %get-tuple-element.207), channel_id=1, source_target_pairs={{0,8},{1,3},{2,10},{3,1},{4,12},{5,7},{6,14},{7,5},{8,0},{9,11},{1... | collective-permute-start | bytes 5111816 | tf_op jit(solution)/shard_map/ppermute | solution.py:931
  177.0 25.9 %copy-start.12 = (bf16[4,832,256]{2,1,0:T(8,128)(2,1)S(1)}, bf16[4,832,256]{2,1,0:T(8,128)(2,1)}, u32[]{:S(2)}) copy-start(bf16[4,832,256]{2,1,0:T(8,128)(2,1)} %get-tuple-element.211.refs_0_.refs_1_) | copy-start | bytes 5111812
  177.0 25.9 %collective-permute-start.15 = (bf16[4,336,256]{2,1,0:T(8,128)(2,1)}, bf16[4,336,256]{2,1,0:T(8,128)(2,1)S(1)}, u32[]{:S(2)}, u32[]{:S(2)}) collective-permute-start(bf16[4,336,256]{2,1,0:T(8,128)(2,1)} %get-tuple-element.208), channel_id=1, source_target_pairs={{0,4},{1,5},{2,6},{3,7},{4,0},{5,1},{6,2},{7,3},{8,12},{9,13},{10,... | collective-permute-start | bytes 2064392 | tf_op jit(solution)/shard_map/ppermute | solution.py:931
  179.0 23.9 %collective-permute-start.16 = (bf16[8,144,256]{2,1,0:T(8,128)(2,1)S(1)}, bf16[8,144,256]{2,1,0:T(8,128)(2,1)S(1)}, u32[]{:S(2)}, u32[]{:S(2)}) collective-permute-start(bf16[8,144,256]{2,1,0:T(8,128)(2,1)S(1)} %bitcast.71), channel_id=1, source_target_pairs={{0,2},{1,5},{2,0},{3,7},{4,6},{5,1},{6,4},{7,3},{8,10},{9,13},{10,... | collective-permute-start | bytes 1769480 | tf_op jit(solution)/shard_map/ppermute | solution.py:931
  179.0 23.9 %collective-permute-start.17 = (bf16[8,64,256]{2,1,0:T(8,128)(2,1)S(1)}, bf16[8,64,256]{2,1,0:T(8,128)(2,1)S(1)}, u32[]{:S(2)}, u32[]{:S(2)}) collective-permute-start(bf16[8,64,256]{2,1,0:T(8,128)(2,1)S(1)} %bitcast.73), channel_id=1, source_target_pairs={{0,8},{1,9},{2,10},{3,11},{4,12},{5,13},{6,14},{7,15},{8,0},{9,1},... | collective-permute-start | bytes 786440 | tf_op jit(solution)/shard_map/ppermute | solution.py:931
  204.0 12.8 %collective-permute-start.18 = (bf16[3,512,512]{2,1,0:T(8,128)(2,1)S(1)}, bf16[3,512,512]{2,1,0:T(8,128)(2,1)S(1)}, u32[]{:S(2)}, u32[]{:S(2)}) collective-permute-start(bf16[3,512,512]{2,1,0:T(8,128)(2,1)S(1)} %slice.103), channel_id=1, source_target_pairs={{0,1},{1,0},{2,3},{3,2},{4,5},{5,4},{6,7},{7,6},{8,9},{9,8},{10,11... | collective-permute-start | bytes 4718600 | tf_op jit(solution)/shard_map/ppermute | solution.py:906
  204.0 12.8 %collective-permute-start.19 = (bf16[2,832,256]{2,1,0:T(8,128)(2,1)S(1)}, bf16[2,832,256]{2,1,0:T(8,128)(2,1)S(1)}, u32[]{:S(2)}, u32[]{:S(2)}) collective-permute-start(bf16[2,832,256]{2,1,0:T(8,128)(2,1)S(1)} %get-tuple-element.215), channel_id=1, source_target_pairs={{0,4},{1,9},{2,6},{3,11},{4,0},{5,13},{6,2},{7,15},{8,12},{9,1},{1... | collective-permute-start | bytes 2555912 | tf_op jit(solution)/shard_map/ppermute | solution.py:931
  205.7 10.2 %collective-permute-start.20 = (bf16[2,336,256]{2,1,0:T(8,128)(2,1)S(1)}, bf16[2,336,256]{2,1,0:T(8,128)(2,1)S(1)}, u32[]{:S(2)}, u32[]{:S(2)}) collective-permute-start(bf16[2,336,256]{2,1,0:T(8,128)(2,1)S(1)} %get-tuple-element.216), channel_id=1, source_target_pairs={{0,2},{1,3},{2,0},{3,1},{4,6},{5,7},{6,4},{7,5},{8,10},{9,11},{10,... | collective-permute-start | bytes 1032200 | tf_op jit(solution)/shard_map/ppermute | solution.py:931
  206.1 17.0 %copy-start.10 = (bf16[1024,1024]{1,0:T(8,128)(2,1)S(1)}, bf16[1024,1024]{1,0:T(8,128)(2,1)}, u32[]{:S(2)}) copy-start(bf16[1024,1024]{1,0:T(8,128)(2,1)} %refs_5_.1) | copy-start | bytes 6291460
  206.1 17.0 %copy-start.22 = (f32[512,1024]{1,0:T(8,128)S(1)}, f32[512,1024]{1,0:T(8,128)}, u32[]{:S(2)}) copy-start(f32[512,1024]{1,0:T(8,128)} %get-tuple-element.167.grad_ref) | copy-start | bytes 6291460
  216.8 23.3 %collective-permute-start.21 = (bf16[8,144,256]{2,1,0:T(8,128)(2,1)S(1)}, bf16[8,144,256]{2,1,0:T(8,128)(2,1)S(1)}, u32[]{:S(2)}, u32[]{:S(2)}) collective-permute-start(bf16[8,144,256]{2,1,0:T(8,128)(2,1)S(1)} %bitcast.72), channel_id=1, source_target_pairs={{0,2},{1,5},{2,0},{3,7},{4,6},{5,1},{6,4},{7,3},{8,10},{9,13},{10,... | collective-permute-start | bytes 1769480 | tf_op jit(solution)/shard_map/ppermute | solution.py:931
  218.2 4.9 %copy-start.6 = (bf16[1024,1024]{1,0:T(8,128)(2,1)S(1)}, bf16[1024,1024]{1,0:T(8,128)(2,1)}, u32[]{:S(2)}) copy-start(bf16[1024,1024]{1,0:T(8,128)(2,1)} %refs_7_.1) | copy-start | bytes 6291460
  218.2 4.9 %copy-start.8 = (bf16[1024,1024]{1,0:T(8,128)(2,1)S(1)}, bf16[1024,1024]{1,0:T(8,128)(2,1)}, u32[]{:S(2)}) copy-start(bf16[1024,1024]{1,0:T(8,128)(2,1)} %refs_6_.1) | copy-start | bytes 6291460
  218.5 10.3 %copy-start.35 = (bf16[1,832,256]{2,1,0:T(8,128)(2,1)}, bf16[1,832,256]{2,1,0:T(8,128)(2,1)S(1)}, u32[]{:S(2)}) copy-start(bf16[1,832,256]{2,1,0:T(8,128)(2,1)S(1)} %get-tuple-element.251.refs_0_) | copy-start | bytes 1277956
  218.5 10.3 %copy-start.37 = (bf16[1,336,256]{2,1,0:T(8,128)(2,1)}, bf16[1,336,256]{2,1,0:T(8,128)(2,1)S(1)}, u32[]{:S(2)}) copy-start(bf16[1,336,256]{2,1,0:T(8,128)(2,1)S(1)} %get-tuple-element.253.refs_2_) | copy-start | bytes 516100
  218.5 21.5 %collective-permute-start.23 = (bf16[1,832,256]{2,1,0:T(8,128)(2,1)S(1)}, bf16[1,832,256]{2,1,0:T(8,128)(2,1)}, u32[]{:S(2)}, u32[]{:S(2)}) collective-permute-start(bf16[1,832,256]{2,1,0:T(8,128)(2,1)S(1)} %get-tuple-element.225), channel_id=1, source_target_pairs={{0,16},{1,17},{2,18},{3,19},{4,20},{5,21},{6,22},{7,23},{8,24},{9,... | collective-permute-start | bytes 1277960 | tf_op jit(solution)/shard_map/ppermute | solution.py:931
  221.5 14.5 %collective-permute-start.22 = (bf16[8,64,256]{2,1,0:T(8,128)(2,1)S(1)}, bf16[8,64,256]{2,1,0:T(8,128)(2,1)}, u32[]{:S(2)}, u32[]{:S(2)}) collective-permute-start(bf16[8,64,256]{2,1,0:T(8,128)(2,1)S(1)} %bitcast.74), channel_id=1, source_target_pairs={{0,8},{1,9},{2,10},{3,11},{4,12},{5,13},{6,14},{7,15},{8,0},{9,1},... | collective-permute-start | bytes 786440 | tf_op jit(solution)/shard_map/ppermute | solution.py:931
  228.8 31.0 %all-to-all-start.2 = ((bf16[8,64,1024]{2,1,0:T(8,128)(2,1)}), bf16[8,64,1024]{2,1,0:T(8,128)(2,1)}, u32[]{:S(2)}, u32[]{:S(2)}) async-start(bf16[8,64,1024]{2,1,0:T(8,128)(2,1)} %bitcast.22), calls=%async_computation.2 | async-start | bytes 2097152 | tf_op jit(solution)/shard_map/all_to_all | solution.py:1007
  233.1 7.0 %copy-start.19 = (bf16[8,3,48,256]{3,2,1,0:T(8,128)(2,1)S(1)}, bf16[8,3,48,256]{3,2,1,0:T(8,128)(2,1)}, u32[]{:S(2)}) copy-start(bf16[8,3,48,256]{3,2,1,0:T(8,128)(2,1)} %copy-done.18) | copy-start | bytes 1769476
  233.1 7.0 %copy-start.21 = (bf16[8,144,256]{2,1,0:T(8,128)(2,1)S(1)}, bf16[8,144,256]{2,1,0:T(8,128)(2,1)}, u32[]{:S(2)}) copy-start(bf16[8,144,256]{2,1,0:T(8,128)(2,1)} %copy-done.20) | copy-start | bytes 1769476
  233.1 7.0 %copy-start.32 = (bf16[8,4,16,256]{3,2,1,0:T(8,128)(2,1)S(1)}, bf16[8,4,16,256]{3,2,1,0:T(8,128)(2,1)}, u32[]{:S(2)}) copy-start(bf16[8,4,16,256]{3,2,1,0:T(8,128)(2,1)} %copy-done.31) | copy-start | bytes 786436
  233.1 7.0 %copy-start.34 = (bf16[8,64,256]{2,1,0:T(8,128)(2,1)S(1)}, bf16[8,64,256]{2,1,0:T(8,128)(2,1)}, u32[]{:S(2)}) copy-start(bf16[8,64,256]{2,1,0:T(8,128)(2,1)} %copy-done.33) | copy-start | bytes 786436
  242.1 13.9 %copy-start.36 = (bf16[1,832,256]{2,1,0:T(8,128)(2,1)S(1)}, bf16[1,832,256]{2,1,0:T(8,128)(2,1)}, u32[]{:S(2)}) copy-start(bf16[1,832,256]{2,1,0:T(8,128)(2,1)} %copy-done.35) | copy-start | bytes 1277956
  242.1 13.9 %copy-start.38 = (bf16[1,336,256]{2,1,0:T(8,128)(2,1)S(1)}, bf16[1,336,256]{2,1,0:T(8,128)(2,1)}, u32[]{:S(2)}) copy-start(bf16[1,336,256]{2,1,0:T(8,128)(2,1)} %copy-done.37) | copy-start | bytes 516100
  242.1 13.6 %collective-permute-start.24 = (bf16[4,288,256]{2,1,0:T(8,128)(2,1)S(1)}, bf16[4,288,256]{2,1,0:T(8,128)(2,1)S(1)}, u32[]{:S(2)}, u32[]{:S(2)}) collective-permute-start(bf16[4,288,256]{2,1,0:T(8,128)(2,1)S(1)} %get-tuple-element.240), channel_id=1, source_target_pairs={{0,8},{1,3},{2,10},{3,1},{4,12},{5,7},{6,14},{7,5},{8,0},{9,11},{1... | collective-permute-start | bytes 1769480 | tf_op jit(solution)/shard_map/ppermute | solution.py:931
  242.8 10.3 %collective-permute-start.25 = (bf16[4,128,256]{2,1,0:T(8,128)(2,1)S(1)}, bf16[4,128,256]{2,1,0:T(8,128)(2,1)S(1)}, u32[]{:S(2)}, u32[]{:S(2)}) collective-permute-start(bf16[4,128,256]{2,1,0:T(8,128)(2,1)S(1)} %get-tuple-element.241), channel_id=1, source_target_pairs={{0,4},{1,5},{2,6},{3,7},{4,0},{5,1},{6,2},{7,3},{8,12},{9,13},{10,... | collective-permute-start | bytes 786440 | tf_op jit(solution)/shard_map/ppermute | solution.py:931
  243.1 9.7 %collective-permute-start.26 = (bf16[1,336,256]{2,1,0:T(8,128)(2,1)S(1)}, bf16[1,336,256]{2,1,0:T(8,128)(2,1)S(1)}, u32[]{:S(2)}, u32[]{:S(2)}) collective-permute-start(bf16[1,336,256]{2,1,0:T(8,128)(2,1)S(1)} %get-tuple-element.242), channel_id=1, source_target_pairs={{0,16},{1,17},{2,18},{3,19},{4,20},{5,21},{6,22},{7,23},{8,24},{9,... | collective-permute-start | bytes 516104 | tf_op jit(solution)/shard_map/ppermute | solution.py:931
  257.9 8.5 %collective-permute-start.30 = (f32[40,2560]{1,0:T(8,128)S(1)}, f32[40,2560]{1,0:T(8,128)S(1)}, u32[]{:S(2)}, u32[]{:S(2)}) collective-permute-start(f32[40,2560]{1,0:T(8,128)S(1)} %get-tuple-element.262), channel_id=1, source_target_pairs={{0,1},{1,0},{2,3},{3,2},{4,5},{5,4},{6,7},{7,6},{8,9},{9,8},{10,11... | collective-permute-start | bytes 1228808 | tf_op jit(solution)/shard_map/ppermute | solution.py:906
  257.9 6.7 %collective-permute-start.27 = (bf16[2,288,256]{2,1,0:T(8,128)(2,1)S(1)}, bf16[2,288,256]{2,1,0:T(8,128)(2,1)S(1)}, u32[]{:S(2)}, u32[]{:S(2)}) collective-permute-start(bf16[2,288,256]{2,1,0:T(8,128)(2,1)S(1)} %get-tuple-element.246), channel_id=1, source_target_pairs={{0,4},{1,9},{2,6},{3,11},{4,0},{5,13},{6,2},{7,15},{8,12},{9,1},{1... | collective-permute-start | bytes 884744 | tf_op jit(solution)/shard_map/ppermute | solution.py:931
  258.3 5.4 %collective-permute-start.28 = (bf16[2,128,256]{2,1,0:T(8,128)(2,1)S(1)}, bf16[2,128,256]{2,1,0:T(8,128)(2,1)S(1)}, u32[]{:S(2)}, u32[]{:S(2)}) collective-permute-start(bf16[2,128,256]{2,1,0:T(8,128)(2,1)S(1)} %get-tuple-element.247), channel_id=1, source_target_pairs={{0,2},{1,3},{2,0},{3,1},{4,6},{5,7},{6,4},{7,5},{8,10},{9,11},{10,... | collective-permute-start | bytes 393224 | tf_op jit(solution)/shard_map/ppermute | solution.py:931
  264.7 12.8 %collective-permute-start.29 = (bf16[1,416,256]{2,1,0:T(8,128)(2,1)S(1)}, bf16[1,416,256]{2,1,0:T(8,128)(2,1)S(1)}, u32[]{:S(2)}, u32[]{:S(2)}) collective-permute-start(bf16[1,416,256]{2,1,0:T(8,128)(2,1)S(1)} %get-tuple-element.260), channel_id=1, source_target_pairs={{0,16},{1,17},{2,18},{3,19},{4,20},{5,21},{6,22},{7,23},{8,24},{9,... | collective-permute-start | bytes 638984 | tf_op jit(solution)/shard_map/ppermute | solution.py:931
  278.1 1.6 collective-permute-start.31
  (25 other events, 49.2 us)
